TPU v7x, 128 devices: a whole 4x4x4 slice. The times are simulated.
128 devices in a mesh: pts: 32 (over y, z, core), tp: 4 (over x).
Axes of the slice: x: 4, y: 4, z: 4, core: 2. Of those that a mesh axis runs over, the one named last changes fastest.
Arguments:
- points: bfloat16 [16384, 512], P('pts'), may hold values from -6 to 6
- destination: int32 [16384, 1], P('pts'), may hold values from 0 to 31; in each aligned block of 512 rows (0 to 511, 512 to 1023, ...) at most 32 rows name the same one
- pattern: int32 [256, 4], P('pts'), may hold values from 0 to 7, as said below
- norm_gain: float32 [512], replicated, may hold values from 0.5 to 1.5
- qkv_weight: bfloat16 [3, 512, 512], P(None, None, 'tp')
- out_weight: bfloat16 [512, 512], P('tp'), may hold values from -0.25 to 0.25
- grad_out: bfloat16 [16384, 512], P('pts'), may hold values from -6 to 6
Outputs:
- out: bfloat16 [16384, 512], P('pts')
- grad_input: bfloat16 [16384, 512], P('pts')
- grad_qkv: float32 [3, 512, 512], P(None, None, 'tp')
- grad_proj: float32 [512, 512], P('tp')
- grad_gain: float32 [512], replicated
Inputs may be any that keep to these rules, and one draw needn't show every extreme that they name: `destination`: among the 512 points of one device no owner is named more than 32 times, and some owner exactly that often. `pattern`: row b of an owner's 8 rows names block b first, then 4 - 1 other distinct blocks of the same window of 1024 slots.
All inputs are finite; a program needn't handle non-finite values.
Results may differ from a plain program's by a relative error of at most 0.035.
Values may be sent and summed in bfloat16 or wider, within the bound.
A program may use at most 64 MiB of HBM per device.

v0:
```python
import jax
import jax.numpy as jnp
from jax import lax
from jax.sharding import PartitionSpec as P

HEADS = 8
BLK = 128
WIN = 1024
KB = 4


def norm_forward(features, norm_gain):
    as_float = features.astype(jnp.float32)
    center = jnp.mean(as_float, -1, keepdims=True)
    shifted = as_float - center
    variance = jnp.mean(shifted * shifted, -1, keepdims=True)
    inv_std = lax.rsqrt(variance + 1e-05)
    x_hat = shifted * inv_std
    return ((x_hat * norm_gain).astype(jnp.bfloat16), x_hat, inv_std)


def norm_backward(grad_normed, x_hat, inv_std, norm_gain):
    grad_float = grad_normed.astype(jnp.float32)
    scaled = grad_float * norm_gain
    first = jnp.mean(scaled, -1, keepdims=True)
    second = jnp.mean(scaled * x_hat, -1, keepdims=True)
    grad_branch = (inv_std * (scaled - first - x_hat * second)).astype(jnp.bfloat16)
    return (grad_branch, jnp.sum(grad_float * x_hat, 0))


def window_probs(queries, key_rows, key_live, query_live, scale):
    scores = (
        jnp.einsum("bqhd,bkhd->bhqk", queries, key_rows, preferred_element_type=jnp.float32) * scale
    )
    query_mask = query_live[:, None, :, None]
    visible = key_live[:, None, None, :] & query_mask
    masked = jnp.where(visible, scores, -1e30)
    top_score = jnp.max(masked, -1, keepdims=True)
    raised = jnp.where(visible, jnp.exp(masked - top_score), 0.0)
    row_total = jnp.sum(raised, -1, keepdims=True)
    return raised / jnp.where(query_mask, row_total, 1.0)


def gather_blocks(rows, plan):
    blocks_win = rows.shape[0] // BLK
    shaped = rows.reshape((blocks_win, BLK) + rows.shape[1:])[plan]
    return shaped.reshape((blocks_win, KB * BLK) + rows.shape[1:])


def window_forward(queries, key_rows, value_rows, live_rows, plan, head_dim):
    blocks_win = WIN // BLK
    heads_here = queries.shape[1]
    query_blocks = queries.reshape(blocks_win, BLK, heads_here, head_dim)
    key_sel = gather_blocks(key_rows, plan)
    value_sel = gather_blocks(value_rows, plan)
    live_sel = gather_blocks(live_rows, plan)
    query_live = live_rows.reshape(blocks_win, BLK)
    attn_probs = window_probs(query_blocks, key_sel, live_sel, query_live, head_dim ** (-0.5))
    probs_low = attn_probs.astype(jnp.bfloat16)
    context = jnp.einsum(
        "bhqk,bkhd->bqhd", probs_low, value_sel, preferred_element_type=jnp.float32
    )
    return context.astype(jnp.bfloat16).reshape(WIN, heads_here * head_dim)


def window_backward(queries, key_rows, value_rows, live_rows, plan, grad_ctx, head_dim):
    blocks_win = WIN // BLK
    heads_here = queries.shape[1]
    query_blocks = queries.reshape(blocks_win, BLK, heads_here, head_dim)
    key_sel = gather_blocks(key_rows, plan)
    value_sel = gather_blocks(value_rows, plan)
    live_sel = gather_blocks(live_rows, plan)
    query_live = live_rows.reshape(blocks_win, BLK)
    scale = head_dim ** (-0.5)
    attn_probs = window_probs(query_blocks, key_sel, live_sel, query_live, scale)
    probs_low = attn_probs.astype(jnp.bfloat16)
    grad_blocks = grad_ctx.reshape(blocks_win, BLK, heads_here, head_dim)
    grad_probs = jnp.einsum(
        "bqhd,bkhd->bhqk", grad_blocks, value_sel, preferred_element_type=jnp.float32
    )
    grad_value_sel = jnp.einsum(
        "bhqk,bqhd->bkhd", probs_low, grad_blocks, preferred_element_type=jnp.float32
    )
    delta = jnp.sum(attn_probs * grad_probs, -1, keepdims=True)
    grad_scores = (attn_probs * (grad_probs - delta) * scale).astype(jnp.bfloat16)
    grad_query = jnp.einsum(
        "bhqk,bkhd->bqhd", grad_scores, key_sel, preferred_element_type=jnp.float32
    ).astype(jnp.bfloat16)
    grad_key_sel = jnp.einsum(
        "bhqk,bqhd->bkhd", grad_scores, query_blocks, preferred_element_type=jnp.float32
    )
    flat_plan = plan.reshape(-1)
    zeros_win = jnp.zeros((blocks_win, BLK, heads_here, head_dim), jnp.float32)
    grad_key = zeros_win.at[flat_plan].add(
        grad_key_sel.reshape(blocks_win * KB, BLK, heads_here, head_dim)
    )
    grad_value = zeros_win.at[flat_plan].add(
        grad_value_sel.reshape(blocks_win * KB, BLK, heads_here, head_dim)
    )
    stacked = jnp.stack(
        [grad_query, grad_key.astype(jnp.bfloat16), grad_value.astype(jnp.bfloat16)], 1
    )
    return stacked.reshape(WIN, 3, heads_here * head_dim)


def owner_plans(pattern, windows):
    blocks_win = WIN // BLK
    offsets = jnp.arange(windows, dtype=jnp.int32) * blocks_win
    return pattern.reshape(windows, blocks_win, KB) - offsets[:, None, None]


def attend(qkv_buf, live, pattern, local_heads):
    slot_count = qkv_buf.shape[0]
    local_width = qkv_buf.shape[2]
    head_dim = local_width // local_heads
    windows = slot_count // WIN
    split = qkv_buf.reshape(windows, WIN, 3, local_heads, head_dim)
    plans = owner_plans(pattern, windows)

    def forward_one(item):
        block_rows, live_rows, plan = item
        return window_forward(
            block_rows[:, 0], block_rows[:, 1], block_rows[:, 2], live_rows, plan, head_dim
        )

    return lax.map(forward_one, (split, live.reshape(windows, WIN), plans)).reshape(
        slot_count, local_width
    )


def attend_back(qkv_buf, live, pattern, grad_buf, local_heads):
    slot_count = qkv_buf.shape[0]
    local_width = qkv_buf.shape[2]
    head_dim = local_width // local_heads
    windows = slot_count // WIN
    split = qkv_buf.reshape(windows, WIN, 3, local_heads, head_dim)
    plans = owner_plans(pattern, windows)
    grad_win = grad_buf.reshape(windows, WIN, local_heads, head_dim)

    def backward_one(item):
        block_rows, live_rows, plan, grad_rows = item
        return window_backward(
            block_rows[:, 0],
            block_rows[:, 1],
            block_rows[:, 2],
            live_rows,
            plan,
            grad_rows,
            head_dim,
        )

    return lax.map(backward_one, (split, live.reshape(windows, WIN), plans, grad_win)).reshape(
        slot_count, 3, local_width
    )


def head_update(context, out_weight):
    term = jnp.dot(context, out_weight, preferred_element_type=jnp.float32)
    return lax.psum(term.astype(jnp.bfloat16), "tp")


def head_normed_grad(grad_qkv_rows, qkv_weight):
    term = jnp.einsum("pjc,jdc->pd", grad_qkv_rows, qkv_weight, preferred_element_type=jnp.float32)
    return lax.psum(term.astype(jnp.bfloat16), "tp")


def body(points, destination, pattern, norm_gain, qkv_weight, out_weight, grad_out):
    pts_count = lax.axis_size("pts")
    point_count = points.shape[0]
    capacity = 2 * point_count // pts_count
    slot_count = pts_count * capacity
    local_heads = HEADS // lax.axis_size("tp")
    target = destination[:, 0]
    onehot = (target[:, None] == jnp.arange(pts_count, dtype=jnp.int32)[None, :]).astype(jnp.int32)
    slot_rank = jnp.sum(jnp.cumsum(onehot, 0) * onehot, 1) - 1
    send_index = target * capacity + slot_rank
    live_source = jnp.ones((point_count,), jnp.bfloat16)

    def place(rows):
        return jnp.zeros((slot_count,) + rows.shape[1:], rows.dtype).at[send_index].set(rows)

    both_rows = jnp.stack([points, grad_out], 1)
    arrived, live_flag = (
        lax.all_to_all(place(both_rows), "pts", split_axis=0, concat_axis=0, tiled=True),
        lax.all_to_all(place(live_source), "pts", split_axis=0, concat_axis=0, tiled=True),
    )
    live = live_flag > 0.5
    owner_points = arrived[:, 0]
    owner_grads = arrived[:, 1]
    normed, x_hat, inv_std = norm_forward(owner_points, norm_gain)
    qkv_rows = jnp.einsum(
        "pd,jdc->pjc", normed, qkv_weight, preferred_element_type=jnp.float32
    ).astype(jnp.bfloat16)
    context = attend(qkv_rows, live, pattern, local_heads)
    update_owner = head_update(context, out_weight)
    update = lax.all_to_all(update_owner, "pts", split_axis=0, concat_axis=0, tiled=True)[
        send_index
    ]
    grad_context = jnp.dot(owner_grads, out_weight.T, preferred_element_type=jnp.float32).astype(
        jnp.bfloat16
    )
    proj_part = jnp.dot(context.T, owner_grads, preferred_element_type=jnp.float32)
    grad_qkv_rows = attend_back(qkv_rows, live, pattern, grad_context, local_heads)
    grad_normed = head_normed_grad(grad_qkv_rows, qkv_weight)
    branch_owner, gain_part = norm_backward(grad_normed, x_hat, inv_std, norm_gain)
    qkv_part = jnp.einsum("pd,pjc->jdc", normed, grad_qkv_rows, preferred_element_type=jnp.float32)
    grad_branch = lax.all_to_all(branch_owner, "pts", split_axis=0, concat_axis=0, tiled=True)[
        send_index
    ]
    out = (points.astype(jnp.float32) + update.astype(jnp.float32)).astype(jnp.bfloat16)
    grad_input = (grad_out.astype(jnp.float32) + grad_branch.astype(jnp.float32)).astype(
        jnp.bfloat16
    )
    grad_qkv, grad_proj, grad_gain = (
        lax.psum(qkv_part.astype(jnp.bfloat16), "pts").astype(jnp.float32),
        lax.psum(proj_part.astype(jnp.bfloat16), "pts").astype(jnp.float32),
        lax.psum(gain_part.astype(jnp.bfloat16), "pts").astype(jnp.float32),
    )
    return (out, grad_input, grad_qkv, grad_proj, grad_gain)


def solution(mesh):
    return jax.shard_map(
        body,
        mesh=mesh,
        in_specs=(
            P("pts", None),
            P("pts", None),
            P("pts", None),
            P(),
            P(None, None, "tp"),
            P("tp", None),
            P("pts", None),
        ),
        out_specs=(P("pts", None), P("pts", None), P(None, None, "tp"), P("tp", None), P()),
        check_vma=False,
    )
```

profile of v0, /device:TPU:0, one launch (start us, length us, event | category | flops | bytes accessed | tf_op | source)
XLA Modules:
  0.0 455.3 jit_solution(16099969647071346106)
XLA Ops:
  11.7 3.8 scatter_custom_fusion.1
  16.1 8.4 %all-to-all-start.1 = ((bf16[32,32,1]{1,2,0:T(2,128)(2,1)}), bf16[32,32,1]{1,2,0:T(2,128)(2,1)S(1)}, u32[]{:S(2)}, u32[]{:S(2)}) async-start(bf16[32,32,1]{1,2,0:T(2,128)(2,1)} %all_to_all.34), calls=%async_computation.1 | async-start | bytes 32768 | tf_op jit(solution)/shard_map/all_to_all | solution.py:185
  28.0 13.6 %scatter_fusion = bf16[1024,2,512]{2,1,0:T(2,128)(2,1)S(1)} fusion(bf16[1024,2,512]{2,1,0:T(2,128)(2,1)S(1)} %broadcast_in_dim.109, s32[512]{0:T(512)S(1)} %bitcast.156, bf16[512,2,512]{2,1,0:T(2,128)(2,1)S(1)} %copy.102), kind=kCustom, calls=%fused_computation.5 | custom fusion | bytes 3147776 | tf_op jit(solution)/shard_map/scatter | solution.py:180
  43.0 7.5 %all-to-all-start = ((bf16[1024,2,512]{2,1,0:T(2,128)(2,1)}), bf16[1024,2,512]{2,1,0:T(2,128)(2,1)S(1)}, u32[]{:S(2)}, u32[]{:S(2)}) async-start(bf16[1024,2,512]{2,1,0:T(2,128)(2,1)} %copy-done.3), calls=%async_computation | async-start | bytes 4194304 | tf_op jit(solution)/shard_map/all_to_all | solution.py:184
  53.5 25.9 %all-to-all-done = bf16[1024,2,512]{2,1,0:T(2,128)(2,1)S(1)} async-done(((bf16[1024,2,512]{2,1,0:T(2,128)(2,1)}), bf16[1024,2,512]{2,1,0:T(2,128)(2,1)S(1)}, u32[]{:S(2)}, u32[]{:S(2)}) %all-to-all-start) | async-done | bytes 2097184 | tf_op jit(solution)/shard_map/all_to_all | solution.py:184
  79.4 4.0 fusion.82
  89.7 4.1 fusion.84
  99.3 2.9 fusion.58
  102.2 16.5 %fusion.43 = bf16[8,1,128,2,64]{2,4,3,0,1:T(8,128)(2,1)S(1)} fusion(f32[8,2,128,512]{3,2,1,0:T(8,128)} %fusion.58, bf16[8,512,2,64]{1,0,3,2:T(8,128)(2,1)S(1)} %reshape.201, f32[8,2,128,512]{3,2,1,0:T(8,128)} %get-tuple-element.78, f32[8,2,128]{2,1,0:T(2,128)S(1)} %copy-done.19), kind=kOutput, calls=%fused_computation.58 | convolution fusion | flops 141691392 | bytes 9707520 | tf_op jit(solution)/shard_map/while/body/eval_jaxpr/bhqk,bkhd->bqhd/dot_general | solution.py:86
  118.7 18.7 %fusion.35 = f32[8,512,2,64]{1,3,2,0:T(8,128)} fusion(f32[8,2,128,512]{3,2,1,0:T(8,128)} %fusion.58, bf16[8,128,2,64]{1,0,3,2:T(8,128)(2,1)S(1)} %bitcast.151, f32[8,2,128,512]{3,2,1,0:T(8,128)} %get-tuple-element.78, f32[8,2,128]{2,1,0:T(2,128)S(1)} %copy-done.19), kind=kOutput, calls=%fused_computation.49 | convolution fusion | flops 141560320 | bytes 10756096 | tf_op jit(solution)/shard_map/while/body/eval_jaxpr/bhqk,bqhd->bkhd/dot_general | solution.py:89
  137.4 4.2 convolution_bitcast_fusion
  146.3 3.0 copy.123
  151.8 2.6 reshape.276
  154.4 4.1 copy.126
  158.6 2.7 scatter_fusion.1
  161.3 4.7 %scatter_fusion.2 = f32[8,128,2,64]{1,3,2,0:T(8,128)S(1)} fusion(f32[8,128,2,64]{1,3,2,0:T(8,128)S(1)} %broadcast.165.clone, s32[32]{0:T(128)S(1)} %copy-done.24, f32[32,128,2,64]{1,3,2,0:T(8,128)} %copy.126), kind=kCustom, calls=%fused_computation.8 | custom fusion | flops 524288 | bytes 6291584 | tf_op jit(solution)/shard_map/while/body/eval_jaxpr/scatter-add | solution.py:97
  174.1 56.3 %all-reduce.7.cloned.1.call-done = (bf16[32,32,512]{2,1,0:T(8,128)(2,1)}, bf16[1024,512]{1,0:T(8,128)(2,1)}) async-done(((bf16[32,32,512]{2,1,0:T(8,128)(2,1)}, bf16[1024,512]{1,0:T(8,128)(2,1)}), (bf16[32,32,512]{2,1,0:T(8,128)(2,1)}, bf16[1024,512]{1,0:T(8,128)(2,1)})) %all-reduce.7.cloned.1.call-update) | async-done | bytes 2097168 | tf_op jit(solution)/shard_map/psum | solution.py:159
  230.3 3.2 fusion.19
  234.5 23.9 %all_to_all.39 = bf16[32,32,512]{2,1,0:T(8,128)(2,1)S(1)} all-to-all(bf16[32,32,512]{2,1,0:T(8,128)(2,1)S(1)} %bitcast.138), channel_id=1, replica_groups=mesh['pts'=32,'tp'=4] {'pts'}, dimensions={0} | all-to-all | bytes 2097152 | tf_op jit(solution)/shard_map/all_to_all | solution.py:207
  258.3 4.2 all-to-all-start.2
  262.6 2.6 convolution_convert_fusion.4
  265.2 2.6 fusion.38
  267.8 103.4 %all-reduce.5.cloned.1.call-done = (bf16[3,512,128]{1,2,0:T(8,128)(2,1)}, bf16[128,512]{1,0:T(8,128)(2,1)}) async-done(((bf16[3,512,128]{1,2,0:T(8,128)(2,1)}, bf16[128,512]{1,0:T(8,128)(2,1)}), (bf16[3,512,128]{1,2,0:T(8,128)(2,1)}, bf16[128,512]{1,0:T(8,128)(2,1)})) %all-reduce.5.cloned.1.call-update) | async-done | bytes 524304 | tf_op jit(solution)/shard_map/psum | solution.py:215
  374.9 66.1 %psum.39 = bf16[512]{0:T(512)(128)(2,1)S(1)} all-reduce(bf16[512]{0:T(512)(128)(2,1)S(1)} %copy-done.23), channel_id=1, replica_groups=mesh['pts'=32,'tp'=4] {'pts'}, use_global_device_ids=true, to_apply=%region_19.20 | all-reduce | flops 512 | bytes 2048 | tf_op jit(solution)/shard_map/psum | solution.py:217
  (132 shorter events, 49.9 us)
Async XLA Ops:
  8.0 88.6 %copy-start = (bf16[128,512]{1,0:T(8,128)(2,1)S(1)}, bf16[128,512]{1,0:T(8,128)(2,1)}, u32[]{:S(2)}) copy-start(bf16[128,512]{1,0:T(8,128)(2,1)} %param.12) | copy-start | bytes 393220
  11.6 16.4 %copy-start.16 = (s32[512,1]{0,1:T(1,128)}, s32[512,1]{0,1:T(1,128)S(1)}, u32[]{:S(2)}) copy-start(s32[512,1]{0,1:T(1,128)S(1)} %compare_select_fusion) | copy-start | bytes 6148
  16.1 26.9 %all-to-all-start.1 = ((bf16[32,32,1]{1,2,0:T(2,128)(2,1)}), bf16[32,32,1]{1,2,0:T(2,128)(2,1)S(1)}, u32[]{:S(2)}, u32[]{:S(2)}) async-start(bf16[32,32,1]{1,2,0:T(2,128)(2,1)} %all_to_all.34), calls=%async_computation.1 | async-start | bytes 32768 | tf_op jit(solution)/shard_map/all_to_all | solution.py:185
  43.0 7.6 %copy-start.10 = (bf16[3,512,128]{2,1,0:T(8,128)(2,1)S(1)}, bf16[3,512,128]{2,1,0:T(8,128)(2,1)}, u32[]{:S(2)}) copy-start(bf16[3,512,128]{2,1,0:T(8,128)(2,1)} %param.11) | copy-start | bytes 1179652
  43.0 7.8 %copy-start.18 = (s32[8,4]{0,1:T(4,128)S(1)}, s32[8,4]{0,1:T(4,128)}, u32[]{:S(2)}) copy-start(s32[8,4]{0,1:T(4,128)} %param.9) | copy-start | bytes 388
  43.0 36.4 %all-to-all-start = ((bf16[1024,2,512]{2,1,0:T(2,128)(2,1)}), bf16[1024,2,512]{2,1,0:T(2,128)(2,1)S(1)}, u32[]{:S(2)}, u32[]{:S(2)}) async-start(bf16[1024,2,512]{2,1,0:T(2,128)(2,1)} %copy-done.3), calls=%async_computation | async-start | bytes 4194304 | tf_op jit(solution)/shard_map/all_to_all | solution.py:184
  50.5 179.8 %all-reduce.7.cloned.1.call-start = ((), (), s32[]{:S(2)}) async-start(), calls=%async_computation.5 | async-start | bytes 4194304 | tf_op jit(solution)/shard_map/psum | solution.py:159
  99.3 2.9 copy-start.19
  102.2 16.5 %copy-start.14 = (bf16[16,8,8,128]{3,2,1,0:T(8,128)(2,1)S(1)}, bf16[16,8,8,128]{3,2,1,0:T(8,128)(2,1)}, u32[]{:S(2)}) copy-start(bf16[16,8,8,128]{3,2,1,0:T(8,128)(2,1)} %copy-done.13) | copy-start | bytes 786436
  137.4 4.2 copy-start.25
  141.6 2.0 copy-start.7
  146.3 3.0 copy-start.6
  154.4 4.2 copy-start.24
  167.4 3.4 copy-start.11
  172.6 57.7 %copy-start.2 = (bf16[1024,1,512]{2,0,1:T(8,128)(2,1)S(1)}, bf16[1024,1,512]{2,0,1:T(8,128)(2,1)}, u32[]{:S(2)}) copy-start(bf16[1024,1,512]{2,0,1:T(8,128)(2,1)} %copy-done.1) | copy-start | bytes 3145732
  172.6 57.7 %copy-start.21 = (f32[512]{0:T(512)S(1)}, f32[512]{0:T(512)}, u32[]{:S(2)}) copy-start(f32[512]{0:T(512)} %param.10) | copy-start | bytes 6148
  230.3 3.3 copy-start.4
  258.3 6.8 %copy-start.22 = (f32[512]{0:T(512)S(1)}, f32[512]{0:T(512)}, u32[]{:S(2)}) copy-start(f32[512]{0:T(512)} %param.10) | copy-start | bytes 6148
  258.3 186.2 %all-to-all-start.2 = ((bf16[32,32,512]{2,1,0:T(8,128)(2,1)}), bf16[32,32,512]{2,1,0:T(8,128)(2,1)S(1)}, u32[]{:S(2)}, u32[]{:S(2)}) async-start(bf16[32,32,512]{2,1,0:T(8,128)(2,1)} %get-tuple-element.68), calls=%async_computation.2 | async-start | bytes 2097152 | tf_op jit(solution)/shard_map/all_to_all | solution.py:196
  262.5 108.7 %all-reduce.5.cloned.1.call-start = ((), (), s32[]{:S(2)}) async-start(), calls=%async_computation.4 | async-start | bytes 1048576 | tf_op jit(solution)/shard_map/psum | solution.py:215
  265.1 2.6 copy-start.17
  265.1 109.8 %copy-start.23 = (bf16[512]{0:T(512)(128)(2,1)S(1)}, bf16[512]{0:T(512)(128)(2,1)}, u32[]{:S(2)}) copy-start(bf16[512]{0:T(512)(128)(2,1)} %get-tuple-element.63) | copy-start | bytes 3076
  441.6 2.0 copy-start.8
  444.5 2.0 copy-start.9
  (7 other events, 7.9 us)
Sparse Core Ops, SparseCore 0:
  174.2 56.0 all-reduce.6
Sparse Core Ops, SparseCore 1:
  267.9 103.3 all-reduce.4
where the time goes:
time: 462 us; the launch traced here: 455 us
  waiting for transfers between devices  186 us (40%)
  blocking collectives  90 us (19%)
  local copies, waits for them, and re-layouts  58.8 us (13%)
  matrix products  56.5 us (12%)
  other arithmetic  27.7 us (6%)
  starting transfers between devices  20.2 us (4%)
  between operations  16.5 us (4%)
    psum x1, waiting for transfers between devices, body(): lax.psum(qkv_part.astype(jnp.bfloat16), 'pts').astype(jnp.float32)  103 us
    psum x1, blocking collectives, body(): lax.psum(gain_part.astype(jnp.bfloat16), 'pts').astype(jnp.float32)  66.1 us
    psum x1, waiting for transfers between devices, head_update(): return lax.psum(term.astype(jnp.bfloat16), 'tp')  56.3 us
    all_to_all x1, waiting for transfers between devices, body(): lax.all_to_all(place(both_rows), 'pts', split_axis=0, concat_axis=0, tile...  25.9 us
    all_to_all x1, blocking collectives, body(): lax.all_to_all(branch_owner, 'pts', split_axis=0, concat_axis=0, tiled=True)  23.9 us
    dot_general x1, matrix products, window_backward(): jnp.einsum('bhqk,bqhd->bkhd', grad_scores, query_blocks, preferred_elemen...  18.7 us
    scatter x2, local copies, waits for them, and re-layouts, place(): jnp.zeros((slot_count,) + rows.shape[1:], rows.dtype).at[send_index]  17.3 us
    dot_general x1, matrix products, window_backward(): jnp.einsum('bhqk,bkhd->bqhd', grad_scores, key_sel, preferred_element_typ...  16.5 us
  transfers between devices with their start and end apart: 5, of which 3 were waited for; matrix products, arithmetic and copies ran while one was open for 7% of the time, Pallas kernels for 0%

commit v1 on v0

v1 whole, which is shorter than its diff:
```python
import functools

import jax
import jax.numpy as jnp
from jax import lax
from jax.experimental import pallas as pl
from jax.experimental.pallas import tpu as pltpu
from jax.sharding import PartitionSpec as P

MESH = pl.DeviceIdType.MESH
F32 = jnp.float32
BF16 = jnp.bfloat16
BLK = 128
NBLK = 8
KB = 4
LANES = 128
HALF = 64
EMPTY = 30000.0
EMPTY_CUT = 10000.0
LOW = -1e30


def nn(a, b):
    return jnp.dot(a, b, preferred_element_type=F32)


def nt(a, b):
    return lax.dot_general(a, b, (((1,), (1,)), ((), ())), preferred_element_type=F32)


def wait_bytes(ref, sem):
    pltpu.make_async_copy(ref, ref, sem).wait()


def kernel(
    n,
    tp,
    pts_ref,
    dest_ref,
    pat_ref,
    gain_ref,
    wqkv_ref,
    wo_ref,
    gout_ref,
    out_ref,
    gin_ref,
    gqkv_ref,
    gproj_ref,
    ggain_ref,
    xhat,
    inv_std,
    normed,
    normed_t,
    gout_t,
    pick,
    rows4,
    a_send,
    a_recv,
    qs,
    gs,
    k_t,
    v_t,
    bias,
    probs,
    dscore,
    stack,
    ra_send,
    ra_recv,
    rb_send,
    rb_recv,
    u_send,
    u_recv,
    n_send,
    n_recv,
    o_all,
    i_all,
    gp_send,
    gp_recv,
    gp_all,
    gw_send,
    gw_recv,
    gw_all,
    gg_recv,
    gx_recv,
    ssem,
    rsem,
):
    me = lax.axis_index("pts")
    tm = lax.axis_index("tp")
    cap = a_send.shape[1]
    per_blk = BLK // cap
    group = me // per_blk
    points = pts_ref.shape[0]
    width = pts_ref.shape[1]
    slots = n * cap
    chunk = points // tp

    def remote(src, dst, phase, peer):
        return pltpu.make_async_remote_copy(
            src_ref=src,
            dst_ref=dst,
            send_sem=ssem.at[phase],
            recv_sem=rsem.at[phase],
            device_id=peer,
            device_id_type=MESH,
        )

    def to_pts(send, recv, phase):
        def one(i, carry):
            peer = lax.rem(me + i, n)
            remote(send(peer), recv.at[me], phase, (peer, tm)).start()
            return carry

        lax.fori_loop(1, n, one, 0)

    def to_tp(send, recv, phase):
        for i in range(1, tp):
            peer = lax.rem(tm + i, tp)
            remote(send(peer), recv.at[tm], phase, (me, peer)).start()

    barrier = pltpu.get_barrier_semaphore()

    def greet(i, carry):
        pl.semaphore_signal(
            barrier, inc=1, device_id=(lax.rem(me + i, n), tm), device_id_type=MESH
        )
        return carry

    lax.fori_loop(1, n, greet, 0)
    for i in range(1, tp):
        pl.semaphore_signal(
            barrier, inc=1, device_id=(me, lax.rem(tm + i, tp)), device_id_type=MESH
        )

    def norm(r, carry):
        at = pl.ds(pl.multiple_of(r * BLK, BLK), BLK)
        x = pts_ref[at, :].astype(F32)
        shifted = x - jnp.mean(x, -1, keepdims=True)
        inv = lax.rsqrt(jnp.mean(shifted * shifted, -1, keepdims=True) + 1e-05)
        hat = shifted * inv
        xhat[at, :] = hat
        inv_std[at, :] = inv
        normed[at, :] = (hat * gain_ref[...]).astype(BF16)
        return carry

    lax.fori_loop(0, points // BLK, norm, 0)
    nm = normed[...]
    rows4[:, 0:LANES] = (nn(nm, wqkv_ref[0]).astype(BF16).astype(F32) * 0.125).astype(BF16)
    rows4[:, LANES : 2 * LANES] = nn(nm, wqkv_ref[1]).astype(BF16)
    rows4[:, 2 * LANES : 3 * LANES] = nn(nm, wqkv_ref[2]).astype(BF16)
    rows4[:, 3 * LANES : 4 * LANES] = nt(gout_ref[...], wo_ref[...]).astype(BF16)

    dest = dest_ref[...].astype(F32)
    lane = lax.broadcasted_iota(jnp.int32, (points, LANES), 1).astype(F32)
    onehot = jnp.where(dest == lane, 1.0, 0.0)
    upto = jnp.where(
        lax.broadcasted_iota(jnp.int32, (points, points), 0)
        >= lax.broadcasted_iota(jnp.int32, (points, points), 1),
        1.0,
        0.0,
    ).astype(BF16)
    count = nn(upto, onehot.astype(BF16))
    index = dest * cap + jnp.sum(count * onehot, -1, keepdims=True) - 1.0
    slot_lane = lax.broadcasted_iota(jnp.int32, (points, slots), 1).astype(F32)
    pick[...] = jnp.where(index == slot_lane, 1.0, 0.0).astype(BF16)
    index_row = jnp.broadcast_to(index, (points, LANES)).T[0:1, :]
    slot_sub = lax.broadcasted_iota(jnp.int32, (BLK, points), 0).astype(F32)
    ones = jnp.ones((points, LANES), BF16)

    pl.semaphore_wait(barrier, n - 1 + tp - 1)

    def place(i, carry):
        c = lax.rem(group + i, NBLK)
        base = (c * BLK).astype(F32)
        put = jnp.where(slot_sub + base == index_row, 1.0, 0.0).astype(BF16)
        live = nn(put, ones)
        qkv = nn(put, rows4[:, 0 : 3 * LANES]).astype(BF16)
        g = jnp.where(live > 0.5, nn(put, rows4[:, 3 * LANES : 4 * LANES]), EMPTY).astype(BF16)
        at = pl.ds(c * per_blk, per_blk)
        a_send[at, :, 0 : 3 * LANES] = qkv.reshape(per_blk, cap, 3 * LANES)
        a_send[at, :, 3 * LANES : 4 * LANES] = g.reshape(per_blk, cap, LANES)
        for u in range(per_blk):
            peer = c * per_blk + u

            @pl.when(peer != me)
            def _():
                remote(a_send.at[peer], a_recv.at[me], 0, (peer, tm)).start()

        return carry

    lax.fori_loop(0, NBLK, place, 0)
    a_recv[me] = a_send[me]

    normed_t[...] = nm.astype(F32).T.astype(BF16)
    gout_t[...] = gout_ref[...].astype(F32).T.astype(BF16)
    probs[:, KB] = jnp.zeros((NBLK, BLK, 2 * BLK), BF16)
    dscore[:, KB] = jnp.zeros((NBLK, BLK, 2 * BLK), BF16)

    wait_bytes(a_recv.at[pl.ds(0, n - 1)], rsem.at[0])

    head_lane = lax.broadcasted_iota(jnp.int32, (BLK, LANES), 1) < HALF

    def prepare(b, carry):
        block = a_recv[pl.ds(b * per_blk, per_blk)].reshape(BLK, 4 * LANES)
        q = block[:, 0:LANES].astype(F32)
        g = block[:, 3 * LANES : 4 * LANES].astype(F32)
        empty = g > EMPTY_CUT
        bias[b] = jnp.where(empty, LOW, 0.0)
        g = jnp.where(empty, 0.0, g)
        qs[b, 0:BLK] = jnp.where(head_lane, q, 0.0).astype(BF16)
        qs[b, BLK : 2 * BLK] = jnp.where(head_lane, 0.0, q).astype(BF16)
        gs[b, 0:BLK] = jnp.where(head_lane, g, 0.0).astype(BF16)
        gs[b, BLK : 2 * BLK] = jnp.where(head_lane, 0.0, g).astype(BF16)
        k_t[b] = block[:, LANES : 2 * LANES].astype(F32).T.astype(BF16)
        v_t[b] = block[:, 2 * LANES : 3 * LANES].astype(F32).T.astype(BF16)
        return carry

    lax.fori_loop(0, NBLK, prepare, 0)

    head_sub = lax.broadcasted_iota(jnp.int32, (LANES, BLK), 0) < HALF

    def send_back(send, recv, phase, b, which):
        for u in which:
            peer = b * per_blk + u

            @pl.when(peer != me)
            def _():
                remote(send.at[peer], recv.at[me], phase, (peer, tm)).start()

    def interleave(b, first, count):
        for j in range(3):
            some = stack[b, pl.ds(3 * cap * first + j, cap * count, stride=3), :]
            rb_send[pl.ds(b * per_blk + first, count), :, j * LANES : (j + 1) * LANES] = (
                some.astype(BF16).reshape(count, cap, LANES)
            )

    def attend(i, carry):
        b = lax.rem(group + i, NBLK)
        chosen = [pat_ref[b, j] for j in range(KB)]

        def keyed(first):
            return jnp.concatenate(
                [
                    a_recv[pl.ds(c * per_blk, per_blk), :, first : first + LANES].reshape(
                        BLK, LANES
                    )
                    for c in chosen
                ],
                0,
            )

        low = jnp.concatenate([bias[c] for c in chosen], 0)
        scores = nt(keyed(LANES), qs[b]) + jnp.concatenate([low, low], 1)
        raised = jnp.exp(scores - jnp.max(scores, 0, keepdims=True))
        p = raised * (1.0 / jnp.sum(raised, 0, keepdims=True))
        dp = nt(keyed(2 * LANES), gs[b])
        delta = jnp.sum(p * dp, 0, keepdims=True)
        ds = (p * (dp - delta)).astype(BF16)
        pb = p.astype(BF16)
        probs[b, 0:KB] = pb.reshape(KB, BLK, 2 * BLK)
        dscore[b, 0:KB] = ds.reshape(KB, BLK, 2 * BLK)
        ctx_t = nn(jnp.concatenate([v_t[c] for c in chosen], 1), pb)
        gq_t = nn(jnp.concatenate([k_t[c] for c in chosen], 1), ds)
        ctx = jnp.where(head_sub, ctx_t[:, 0:BLK], ctx_t[:, BLK : 2 * BLK]).T
        gq = jnp.where(head_sub, gq_t[:, 0:BLK], gq_t[:, BLK : 2 * BLK]).T * 0.125
        at = pl.ds(b * per_blk, per_blk)
        ra_send[at] = ctx.astype(BF16).reshape(per_blk, cap, LANES)
        send_back(ra_send, ra_recv, 1, b, range(per_blk))
        stack[b, 0:BLK] = gq
        interleave(b, 0, 1)
        send_back(rb_send, rb_recv, 2, b, range(1))
        return carry

    lax.fori_loop(0, NBLK, attend, 0)
    ra_recv[me] = ra_send[me]

    def attend_keys(i, carry):
        c = lax.rem(group + i, NBLK)
        gk = jnp.zeros((BLK, LANES), F32)
        gv = jnp.zeros((BLK, LANES), F32)
        for b in range(NBLK):
            j = jnp.int32(KB)
            for which in range(KB):
                j = jnp.where(pat_ref[b, which] == c, which, j)
            gk = gk + nn(dscore[b, j], qs[b])
            gv = gv + nn(probs[b, j], gs[b])
        stack[c, BLK : 2 * BLK] = gk
        stack[c, 2 * BLK : 3 * BLK] = gv
        interleave(c, 1, per_blk - 1)
        send_back(rb_send, rb_recv, 2, c, range(1, per_blk))
        return carry

    lax.fori_loop(0, NBLK, attend_keys, 0)
    rb_recv[me] = rb_send[me]

    wait_bytes(ra_recv.at[pl.ds(0, n - 1)], rsem.at[1])
    context = nn(pick[...], ra_recv[...].reshape(slots, LANES)).astype(BF16)
    u_send[...] = nn(context, wo_ref[...]).astype(BF16).reshape(tp, chunk, width)
    to_tp(lambda peer: u_send.at[peer], u_recv, 3)
    gp_send[...] = nn(gout_t[...], context).astype(BF16).reshape(gp_send.shape)
    to_pts(lambda peer: gp_send.at[peer], gp_recv, 4)

    mine = pl.ds(pl.multiple_of(tm * chunk, chunk), chunk)
    u_recv[tm] = u_send[tm]
    wait_bytes(u_recv.at[pl.ds(0, tp - 1)], rsem.at[3])
    update = jnp.sum(u_recv[...].astype(F32), 0).astype(BF16).astype(F32)
    o_all[tm] = (pts_ref[mine, :].astype(F32) + update).astype(BF16)
    to_tp(lambda peer: o_all.at[tm], o_all, 5)

    gp_recv[me] = gp_send[me]
    wait_bytes(gp_recv.at[pl.ds(0, n - 1)], rsem.at[4])
    gp_all[me] = jnp.sum(gp_recv[...].astype(F32), 0).astype(BF16)
    to_pts(lambda peer: gp_all.at[me], gp_all, 6)

    wait_bytes(rb_recv.at[pl.ds(0, n - 1)], rsem.at[2])
    back = nn(pick[...], rb_recv[...].reshape(slots, 3 * LANES)).astype(BF16)
    gq = back[:, 0:LANES]
    gk = back[:, LANES : 2 * LANES]
    gv = back[:, 2 * LANES : 3 * LANES]
    part = nt(gq, wqkv_ref[0]) + nt(gk, wqkv_ref[1]) + nt(gv, wqkv_ref[2])
    n_send[...] = part.astype(BF16).reshape(tp, chunk, width)
    to_tp(lambda peer: n_send.at[peer], n_recv, 7)
    nmt = normed_t[...]
    grads = jnp.concatenate([nn(nmt, gq), nn(nmt, gk), nn(nmt, gv)], 0)
    gw_send[...] = grads.astype(BF16).reshape(gw_send.shape)
    to_pts(lambda peer: gw_send.at[peer], gw_recv, 8)
    gain_part = jnp.sum(part * xhat[...], 0, keepdims=True)
    for j in range(width // LANES):
        gg_recv[me, j] = gain_part[:, j * LANES : (j + 1) * LANES]
    to_pts(lambda peer: gg_recv.at[me], gg_recv, 9)

    n_recv[tm] = n_send[tm]
    wait_bytes(n_recv.at[pl.ds(0, tp - 1)], rsem.at[7])
    grad = jnp.sum(n_recv[...].astype(F32), 0).astype(BF16).astype(F32)
    hat = xhat[mine, :]
    scaled = grad * gain_ref[...]
    first = jnp.mean(scaled, -1, keepdims=True)
    second = jnp.mean(scaled * hat, -1, keepdims=True)
    branch = (inv_std[mine, :] * (scaled - first - hat * second)).astype(BF16).astype(F32)
    i_all[tm] = (gout_ref[mine, :].astype(F32) + branch).astype(BF16)
    to_tp(lambda peer: i_all.at[tm], i_all, 10)

    gw_recv[me] = gw_send[me]
    wait_bytes(gw_recv.at[pl.ds(0, n - 1)], rsem.at[8])
    gw_all[me] = jnp.sum(gw_recv[...].astype(F32), 0).astype(BF16)
    to_pts(lambda peer: gw_all.at[me], gw_all, 11)

    wait_bytes(gg_recv.at[pl.ds(0, n - 1)], rsem.at[9])
    gx_recv[tm] = jnp.sum(gg_recv[...], 0)
    to_tp(lambda peer: gx_recv.at[tm], gx_recv, 12)

    wait_bytes(o_all.at[pl.ds(0, tp - 1)], rsem.at[5])
    out_ref[...] = o_all[...].reshape(points, width)
    wait_bytes(gp_all.at[pl.ds(0, n - 1)], rsem.at[6])
    proj_t = gp_all[...].reshape(width, LANES).astype(F32)
    gproj_ref[...] = proj_t.T
    wait_bytes(i_all.at[pl.ds(0, tp - 1)], rsem.at[10])
    gin_ref[...] = i_all[...].reshape(points, width)
    wait_bytes(gx_recv.at[pl.ds(0, tp - 1)], rsem.at[12])
    gain_sum = jnp.sum(gx_recv[...], 0)
    for j in range(width // LANES):
        ggain_ref[:, j * LANES : (j + 1) * LANES] = gain_sum[j]
    wait_bytes(gw_all.at[pl.ds(0, n - 1)], rsem.at[11])
    gqkv_ref[...] = gw_all[...].reshape(gqkv_ref.shape).astype(F32)

    pts_bufs = ((0, a_send), (1, ra_send), (2, rb_send), (4, gp_send), (6, gp_all))
    pts_bufs += ((8, gw_send), (9, gg_recv), (11, gw_all))
    for phase, buf in pts_bufs:
        wait_bytes(buf.at[pl.ds(0, n - 1)], ssem.at[phase])
    for phase, buf in ((3, u_send), (5, o_all), (7, n_send), (10, i_all), (12, gx_recv)):
        wait_bytes(buf.at[pl.ds(0, tp - 1)], ssem.at[phase])


def body(n, tp, points, destination, pattern, norm_gain, qkv_weight, out_weight, grad_out):
    rows, width = points.shape
    cap = 2 * rows // n
    slots = n * cap
    chunk = rows // tp
    wrows = 3 * width // n
    prows = width // n
    vm = pl.BlockSpec(memory_space=pltpu.VMEM)
    scratch = [
        pltpu.VMEM((rows, width), F32),
        pltpu.VMEM((rows, 1), F32),
        pltpu.VMEM((rows, width), BF16),
        pltpu.VMEM((width, rows), BF16),
        pltpu.VMEM((width, rows), BF16),
        pltpu.VMEM((rows, slots), BF16),
        pltpu.VMEM((rows, 4 * LANES), BF16),
        pltpu.VMEM((n, cap, 4 * LANES), BF16),
        pltpu.VMEM((n, cap, 4 * LANES), BF16),
        pltpu.VMEM((NBLK, 2 * BLK, LANES), BF16),
        pltpu.VMEM((NBLK, 2 * BLK, LANES), BF16),
        pltpu.VMEM((NBLK, LANES, BLK), BF16),
        pltpu.VMEM((NBLK, LANES, BLK), BF16),
        pltpu.VMEM((NBLK, BLK, LANES), F32),
        pltpu.VMEM((NBLK, KB + 1, BLK, 2 * BLK), BF16),
        pltpu.VMEM((NBLK, KB + 1, BLK, 2 * BLK), BF16),
        pltpu.VMEM((NBLK, 3 * BLK, LANES), F32),
        pltpu.VMEM((n, cap, LANES), BF16),
        pltpu.VMEM((n, cap, LANES), BF16),
        pltpu.VMEM((n, cap, 3 * LANES), BF16),
        pltpu.VMEM((n, cap, 3 * LANES), BF16),
        pltpu.VMEM((tp, chunk, width), BF16),
        pltpu.VMEM((tp, chunk, width), BF16),
        pltpu.VMEM((tp, chunk, width), BF16),
        pltpu.VMEM((tp, chunk, width), BF16),
        pltpu.VMEM((tp, chunk, width), BF16),
        pltpu.VMEM((tp, chunk, width), BF16),
        pltpu.VMEM((n, prows, LANES), BF16),
        pltpu.VMEM((n, prows, LANES), BF16),
        pltpu.VMEM((n, prows, LANES), BF16),
        pltpu.VMEM((n, wrows, LANES), BF16),
        pltpu.VMEM((n, wrows, LANES), BF16),
        pltpu.VMEM((n, wrows, LANES), BF16),
        pltpu.VMEM((n, width // LANES, 1, LANES), F32),
        pltpu.VMEM((tp, width // LANES, 1, LANES), F32),
        pltpu.SemaphoreType.DMA((13,)),
        pltpu.SemaphoreType.DMA((13,)),
    ]
    out, grad_input, grad_qkv, grad_proj, grad_gain = pl.pallas_call(
        functools.partial(kernel, n, tp),
        out_shape=(
            jax.ShapeDtypeStruct((rows, width), BF16),
            jax.ShapeDtypeStruct((rows, width), BF16),
            jax.ShapeDtypeStruct((3, width, LANES), F32),
            jax.ShapeDtypeStruct((LANES, width), F32),
            jax.ShapeDtypeStruct((1, width), F32),
        ),
        in_specs=[vm, vm, pl.BlockSpec(memory_space=pltpu.SMEM), vm, vm, vm, vm],
        out_specs=(vm,) * 5,
        scratch_shapes=scratch,
        compiler_params=pltpu.CompilerParams(
            collective_id=0, has_side_effects=True, vmem_limit_bytes=48 * 1024 * 1024
        ),
        name="point_attention",
    )(
        points,
        destination,
        pattern,
        norm_gain.reshape(1, width),
        qkv_weight,
        out_weight,
        grad_out,
    )
    return out, grad_input, grad_qkv, grad_proj, grad_gain.reshape(width)


def solution(mesh):
    return jax.shard_map(
        functools.partial(body, mesh.shape["pts"], mesh.shape["tp"]),
        mesh=mesh,
        in_specs=(
            P("pts", None),
            P("pts", None),
            P("pts", None),
            P(),
            P(None, None, "tp"),
            P("tp", None),
            P("pts", None),
        ),
        out_specs=(P("pts", None), P("pts", None), P(None, None, "tp"), P("tp", None), P()),
        check_vma=False,
    )
```

time: 462 us -> 81.4 us (0.18); the launches traced: 455 us -> 81 us
  waiting for transfers between devices: 186 us -> 0 us
  blocking collectives: 90 us -> 0 us
  Pallas kernels: 0 us -> 71.8 us
  matrix products: 56.5 us -> 0 us
  local copies, waits for them, and re-layouts: 58.8 us -> 8.49 us
  other arithmetic: 27.7 us -> 0 us
  starting transfers between devices: 20.2 us -> 0 us
  between operations: 16.5 us -> 0.66 us
    psum x2 -> x0, waiting for transfers between devices: 160 us -> none  [the longest x1 103 us: body(): lax.psum(qkv_part.astype(jnp.bfloat16), 'pts').astype(jnp.float32)]
    pallas_call x0 -> x1, Pallas kernels: none -> 71.8 us  [body(): pl.pallas_call(functools.partial(kernel, n, tp), out_shape=(jax.ShapeDtyp...]
    psum x1 -> x0, blocking collectives: 66.1 us -> none  [body(): lax.psum(gain_part.astype(jnp.bfloat16), 'pts').astype(jnp.float32)]
    dot_general x11 -> x0, matrix products: 55.7 us -> none  [the longest x1 18.7 us: window_backward(): jnp.einsum('bhqk,bqhd->bkhd', grad_scores, query_blocks, preferred_elemen...]
    all_to_all x3 -> x0, waiting for transfers between devices: 25.9 us -> none  [the longest x1 25.9 us: body(): lax.all_to_all(place(both_rows), 'pts', split_axis=0, concat_axis=0, tile...]
    all_to_all x1 -> x0, blocking collectives: 23.9 us -> none  [body(): lax.all_to_all(branch_owner, 'pts', split_axis=0, concat_axis=0, tiled=True)]
    all_to_all x3 -> x0, starting transfers between devices: 20.1 us -> none  [the longest x1 8.42 us: body(): lax.all_to_all(place(live_source), 'pts', split_axis=0, concat_axis=0, ti...]
    scatter x2 -> x0, local copies, waits for them, and re-layouts: 17.3 us -> none  [place(): jnp.zeros((slot_count,) + rows.shape[1:], rows.dtype).at[send_index]]
  transfers between devices with their start and end apart: 5 -> 0, of which waited for: 3 -> 0; matrix products, arithmetic and copies ran while one was open for 7% -> 0% of each run, Pallas kernels for 0% -> 0%
where the time goes in v1:
time: 81.4 us; the launch traced here: 81 us
  Pallas kernels  71.8 us (88%)
  local copies, waits for them, and re-layouts  8.49 us (10%)
    pallas_call x1, Pallas kernels, body(): pl.pallas_call(functools.partial(kernel, n, tp), out_shape=(jax.ShapeDtyp...  71.8 us
    unnamed x19, local copies, waits for them, and re-layouts  8.49 us

profile of v1, /device:TPU:0, one launch (start us, length us, event | category | flops | bytes accessed | tf_op | source)
XLA Modules:
  0.0 81.0 jit_solution(2772887927603154341)
XLA Ops:
  0.6 0.0 copy-start.5
  0.6 0.8 copy.13.pat_ref
  1.4 0.0 copy-done.5
  1.4 0.0 copy-start.3
  1.4 0.0 copy-start.4
  1.4 0.1 copy.12.dest_ref
  1.6 0.7 copy-done.3
  2.3 0.0 copy-done.4
  2.3 0.0 copy-start
  2.3 1.0 %copy-done = bf16[512,512]{1,0:T(8,128)(2,1)S(1)} copy-done((bf16[512,512]{1,0:T(8,128)(2,1)S(1)}, bf16[512,512]{1,0:T(8,128)(2,1)}, u32[]{:S(2)}) %copy-start) | copy-done | bytes 524312
  3.4 0.0 copy-start.1
  3.4 1.0 %copy-done.1 = bf16[512,512]{1,0:T(8,128)(2,1)S(1)} copy-done((bf16[512,512]{1,0:T(8,128)(2,1)S(1)}, bf16[512,512]{1,0:T(8,128)(2,1)}, u32[]{:S(2)}) %copy-start.1) | copy-done | bytes 524312
  4.4 0.0 copy-start.2
  4.4 1.0 %copy-done.2 = bf16[3,512,128]{2,1,0:T(8,128)(2,1)S(1)} copy-done((bf16[3,512,128]{2,1,0:T(8,128)(2,1)S(1)}, bf16[3,512,128]{2,1,0:T(8,128)(2,1)}, u32[]{:S(2)}) %copy-start.2) | copy-done | bytes 393240
  5.4 71.8 %point_attention.1 = (bf16[512,512]{1,0:T(8,128)(2,1)S(1)}, bf16[512,512]{1,0:T(8,128)(2,1)S(1)}, f32[3,512,128]{2,1,0:T(8,128)S(1)}, f32[128,512]{1,0:T(8,128)S(1)}, f32[1,512]{1,0:T(1,128)S(1)}) custom-call(bf16[512,512]{1,0:T(8,128)(2,1)S(1)} %copy-done, s32[512,1]{1,0:T(8,128)S(1)} %copy.12.dest_ref, s32[8,4]{1,0:T(8,128)S(1)} %copy.13.pat_ref, ...), custom_call_target="tpu_custom_call" | custom-call | tf_op jit(solution)/shard_map/point_attention/pallas_call | solution.py:421
  77.2 0.8 copy.19
  78.0 0.8 copy.20
  78.8 0.9 %copy.21 = f32[3,512,128]{2,1,0:T(8,128)} copy(f32[3,512,128]{2,1,0:T(8,128)S(1)} %get-tuple-element.22) | data formatting | bytes 1572864
  79.7 0.7 copy.22
  80.4 0.6 copy.23
Async XLA Ops:
  0.6 0.8 copy-start.5
  1.4 0.9 %copy-start.3 = (bf16[128,512]{1,0:T(8,128)(2,1)S(1)}, bf16[128,512]{1,0:T(8,128)(2,1)}, u32[]{:S(2)}) copy-start(bf16[128,512]{1,0:T(8,128)(2,1)} %wo_ref.1) | copy-start | bytes 393220
  1.4 0.9 %copy-start.4 = (f32[512]{0:T(512)S(1)}, f32[512]{0:T(512)}, u32[]{:S(2)}) copy-start(f32[512]{0:T(512)} %param.10) | copy-start | bytes 6148
  2.3 1.0 %copy-start = (bf16[512,512]{1,0:T(8,128)(2,1)S(1)}, bf16[512,512]{1,0:T(8,128)(2,1)}, u32[]{:S(2)}) copy-start(bf16[512,512]{1,0:T(8,128)(2,1)} %pts_ref.1) | copy-start | bytes 1572868
  3.4 1.0 %copy-start.1 = (bf16[512,512]{1,0:T(8,128)(2,1)S(1)}, bf16[512,512]{1,0:T(8,128)(2,1)}, u32[]{:S(2)}) copy-start(bf16[512,512]{1,0:T(8,128)(2,1)} %gout_ref.1) | copy-start | bytes 1572868
  4.4 1.0 %copy-start.2 = (bf16[3,512,128]{2,1,0:T(8,128)(2,1)S(1)}, bf16[3,512,128]{2,1,0:T(8,128)(2,1)}, u32[]{:S(2)}) copy-start(bf16[3,512,128]{2,1,0:T(8,128)(2,1)} %wqkv_ref.1) | copy-start | bytes 1179652

commit v2 on v1

v2 whole, which is shorter than its diff:
```python
import functools

import jax
import jax.numpy as jnp
from jax import lax
from jax.experimental import pallas as pl
from jax.experimental.pallas import tpu as pltpu
from jax.sharding import PartitionSpec as P

MESH = pl.DeviceIdType.MESH
F32 = jnp.float32
BF16 = jnp.bfloat16
BLK = 128
NBLK = 8
KB = 4
LANES = 128
HALF = 64
EMPTY = 2e38
EMPTY_CUT = 1e38
LOW = -1e30
VMEM_LIMIT = 60 * 1024 * 1024
YS, ZS, CORES = 4, 4, 2


def ring(step, size):
    return min(step, size - step)


OFFSETS = sorted(
    [(y, z, c) for y in range(YS) for z in range(ZS) for c in range(CORES)][1:],
    key=lambda o: (-ring(o[0], YS) - ring(o[1], ZS), o),
)

(K_Q, K_V, K_G, K_CTX, K_BACK, K_UPD, K_OUT, K_N0, K_N1, K_I0, K_I1, K_W, K_WALL, K_GAIN, K_GAINX) = (
    range(15)
)


def nn(a, b):
    return jnp.dot(a, b, preferred_element_type=F32)


def nt(a, b):
    return lax.dot_general(a, b, (((1,), (1,)), ((), ())), preferred_element_type=F32)


def wait_bytes(ref, sem):
    pltpu.make_async_copy(ref, ref, sem).wait()


def kernel(
    n,
    tp,
    pts_hbm,
    dest_hbm,
    pat_hbm,
    gain_hbm,
    wqkv_hbm,
    wo_hbm,
    gout_hbm,
    out_ref,
    gin_ref,
    gqkv_ref,
    gproj_ref,
    ggain_ref,
    pts_ref,
    dest_ref,
    pat_ref,
    gain_ref,
    wqkv_ref,
    wo_ref,
    gout_ref,
    in_sem,
    xhat,
    inv_std,
    normed,
    normed_t,
    gout_t,
    pick,
    put_all,
    rows_kq,
    rows_vg,
    kq_send,
    kq_recv,
    v_send,
    v_recv,
    g_send,
    g_recv,
    qs,
    gs,
    k_t,
    v_t,
    bias,
    probs,
    gk_part,
    gv_part,
    stack,
    ra_send,
    ra_recv,
    rb_send,
    rb_recv,
    u_send,
    u_recv,
    n_send,
    n_recv,
    o_all,
    i_all,
    gw_send,
    gw_recv,
    gw_all,
    gg_recv,
    gx_recv,
    ssem,
    rsem,
):
    me = lax.axis_index("pts")
    tm = lax.axis_index("tp")
    cap = kq_send.shape[1]
    per_blk = BLK // cap
    points, width = pts_ref.shape
    slots = n * cap
    chunk = points // tp
    half = chunk // 2
    my_y = me // (ZS * CORES)
    my_z = lax.rem(me // CORES, ZS)
    my_c = lax.rem(me, CORES)

    barrier = pltpu.get_barrier_semaphore()

    def greet(i, carry):
        pl.semaphore_signal(
            barrier, inc=1, device_id=(lax.rem(me + i, n), tm), device_id_type=MESH
        )
        return carry

    for i in range(1, tp):
        pl.semaphore_signal(
            barrier, inc=1, device_id=(me, lax.rem(tm + i, tp)), device_id_type=MESH
        )
    lax.fori_loop(1, n, greet, 0)

    fetches = [
        pltpu.make_async_copy(src, dst, in_sem.at[i])
        for i, (src, dst) in enumerate(
            (
                (dest_hbm, dest_ref),
                (pts_hbm, pts_ref),
                (gain_hbm, gain_ref),
                (wqkv_hbm, wqkv_ref),
                (gout_hbm, gout_ref),
                (wo_hbm, wo_ref),
                (pat_hbm, pat_ref),
            )
        )
    ]
    for fetch in fetches:
        fetch.start()

    def remote(src, dst, phase, peer):
        return pltpu.make_async_remote_copy(
            src_ref=src,
            dst_ref=dst,
            send_sem=ssem.at[phase],
            recv_sem=rsem.at[phase],
            device_id=peer,
            device_id_type=MESH,
        )

    def to_pts(send, recv, phase):
        for dy, dz, dc in OFFSETS:
            peer = (lax.rem(my_y + dy, YS) * ZS + lax.rem(my_z + dz, ZS)) * CORES
            peer = peer + lax.rem(my_c + dc, CORES)
            remote(send(peer), recv.at[me], phase, (peer, tm)).start()

    def to_tp(send, recv, phase):
        for i in range(1, tp):
            peer = lax.rem(tm + i, tp)
            remote(send(peer), recv(tm), phase, (me, peer)).start()

    def nth(i):
        dy = jnp.where(i < 2, 2, jnp.where(i < 6, 1 + 2 * lax.rem(i, 2), 0))
        dz = jnp.where(i < 2, 1 - i, jnp.where(i < 6, 1 - (i - 2) // 2, 7 - i))
        return lax.rem(my_y + dy, YS) * 2 + lax.rem(my_z // 2 + dz, 2)

    def to_group(send, recv, phase, b, which):
        for u in which:
            peer = b * per_blk + u

            @pl.when(peer != me)
            def _():
                remote(send.at[peer], recv.at[me], phase, (peer, tm)).start()

    upto = jnp.where(
        lax.broadcasted_iota(jnp.int32, (points, points), 0)
        <= lax.broadcasted_iota(jnp.int32, (points, points), 1),
        1.0,
        0.0,
    ).astype(BF16)
    fetches[0].wait()
    dest = dest_ref[...].astype(F32)
    owner = lax.broadcasted_iota(jnp.int32, (n, points), 0).astype(F32)
    onehot = jnp.where(dest == owner, 1.0, 0.0)
    count = nn(onehot.astype(BF16), upto)
    index = dest * cap + jnp.sum(count * onehot, 0, keepdims=True) - 1.0

    fetches[1].wait()
    fetches[2].wait()

    def norm(r, carry):
        at = pl.ds(pl.multiple_of(r * BLK, BLK), BLK)
        x = pts_ref[at, :].astype(F32)
        shifted = x - jnp.mean(x, -1, keepdims=True)
        inv = lax.rsqrt(jnp.mean(shifted * shifted, -1, keepdims=True) + 1e-05)
        hat = shifted * inv
        xhat[at, :] = hat
        inv_std[at, :] = inv
        normed[at, :] = (hat * gain_ref[...]).astype(BF16)
        return carry

    lax.fori_loop(0, points // BLK, norm, 0)
    fetches[3].wait()
    nm = normed[...]
    rows_kq[:, 0:LANES] = nn(nm, wqkv_ref[1]).astype(BF16)
    rows_kq[:, LANES : 2 * LANES] = (nn(nm, wqkv_ref[0]).astype(BF16).astype(F32) * 0.125).astype(
        BF16
    )
    slot_sub = lax.broadcasted_iota(jnp.int32, (BLK, points), 0).astype(F32)
    ones = jnp.ones((points, LANES), BF16)

    pl.semaphore_wait(barrier, n - 1 + tp - 1)

    def place(i, carry):
        c = nth(i)
        base = (c * BLK).astype(F32)
        put = jnp.where(slot_sub + base == index, 1.0, 0.0).astype(BF16)
        put_all[c] = put
        live = nn(put, ones)
        kq = nn(put, rows_kq[...])
        k = kq[:, 0:LANES].astype(BF16)
        q = jnp.where(live > 0.5, kq[:, LANES : 2 * LANES], EMPTY).astype(BF16)
        at = pl.ds(c * per_blk, per_blk)
        kq_send[at, :, 0:LANES] = k.reshape(per_blk, cap, LANES)
        kq_send[at, :, LANES : 2 * LANES] = q.reshape(per_blk, cap, LANES)
        to_group(kq_send, kq_recv, K_Q, c, range(per_blk))
        return carry

    lax.fori_loop(0, NBLK, place, 0)
    kq_recv[me] = kq_send[me]

    fetches[4].wait()
    fetches[5].wait()
    rows_vg[:, 0:LANES] = nn(nm, wqkv_ref[2]).astype(BF16)
    rows_vg[:, LANES : 2 * LANES] = nt(gout_ref[...], wo_ref[...]).astype(BF16)

    def place_more(i, carry):
        c = nth(i)
        vg = nn(put_all[c], rows_vg[...]).astype(BF16)
        at = pl.ds(c * per_blk, per_blk)
        v_send[at] = vg[:, 0:LANES].reshape(per_blk, cap, LANES)
        g_send[at] = vg[:, LANES : 2 * LANES].reshape(per_blk, cap, LANES)
        to_group(v_send, v_recv, K_V, c, range(per_blk))
        return carry

    lax.fori_loop(0, NBLK, place_more, 0)
    to_pts(lambda peer: g_send.at[peer], g_recv, K_G)
    v_recv[me] = v_send[me]
    g_recv[me] = g_send[me]

    fetches[6].wait()
    index_col = jnp.broadcast_to(index, (LANES, points)).T
    lane = lax.broadcasted_iota(jnp.int32, (points, LANES), 1).astype(F32)
    for t in range(slots // LANES):
        pick[:, t * LANES : (t + 1) * LANES] = jnp.where(
            index_col == lane + t * LANES, 1.0, 0.0
        ).astype(BF16)
    normed_t[...] = nm.astype(F32).T.astype(BF16)
    gout_t[...] = gout_ref[...].astype(F32).T.astype(BF16)
    gk_part[:, KB] = jnp.zeros((NBLK, BLK, LANES), F32)
    gv_part[:, KB] = jnp.zeros((NBLK, BLK, LANES), F32)

    head_lane = lax.broadcasted_iota(jnp.int32, (BLK, LANES), 1) < HALF
    head_sub = lax.broadcasted_iota(jnp.int32, (LANES, BLK), 0) < HALF

    def block_of(ref, b, first=0):
        return ref[pl.ds(b * per_blk, per_blk), :, first : first + LANES].reshape(BLK, LANES)

    def halves(ref, b, rows):
        ref[b, 0:BLK] = jnp.where(head_lane, rows, 0.0).astype(BF16)
        ref[b, BLK : 2 * BLK] = jnp.where(head_lane, 0.0, rows).astype(BF16)

    def chosen_of(b):
        return [pat_ref[j, b] for j in range(KB)]

    wait_bytes(kq_recv.at[pl.ds(0, n - 1)], rsem.at[K_Q])

    def prepare(b, carry):
        q = block_of(kq_recv, b, LANES).astype(F32)
        empty = q > EMPTY_CUT
        bias[b] = jnp.where(empty, LOW, 0.0)
        halves(qs, b, jnp.where(empty, 0.0, q))
        k_t[b] = block_of(kq_recv, b).astype(F32).T.astype(BF16)
        return carry

    lax.fori_loop(0, NBLK, prepare, 0)

    def softmax(b, carry):
        chosen = chosen_of(b)
        keys = jnp.concatenate([block_of(kq_recv, c) for c in chosen], 0)
        low = jnp.concatenate([bias[c] for c in chosen], 0)
        scores = nt(keys, qs[b]) + jnp.concatenate([low, low], 1)
        raised = jnp.exp(scores - jnp.max(scores, 0, keepdims=True))
        p = raised * (1.0 / jnp.sum(raised, 0, keepdims=True))
        probs[b] = p.astype(BF16)
        return carry

    lax.fori_loop(0, NBLK, softmax, 0)

    wait_bytes(v_recv.at[pl.ds(0, n - 1)], rsem.at[K_V])

    def prepare_v(b, carry):
        v_t[b] = block_of(v_recv, b).astype(F32).T.astype(BF16)
        return carry

    lax.fori_loop(0, NBLK, prepare_v, 0)

    def mix(i, carry):
        b = nth(i)
        values_t = jnp.concatenate([v_t[c] for c in chosen_of(b)], 1)
        ctx_t = nn(values_t, probs[b])
        ctx = jnp.where(head_sub, ctx_t[:, 0:BLK], ctx_t[:, BLK : 2 * BLK]).T
        at = pl.ds(b * per_blk, per_blk)
        ra_send[at] = ctx.astype(BF16).reshape(per_blk, cap, LANES)
        to_group(ra_send, ra_recv, K_CTX, b, range(per_blk))
        return carry

    lax.fori_loop(0, NBLK, mix, 0)
    ra_recv[me] = ra_send[me]

    wait_bytes(g_recv.at[pl.ds(0, n - 1)], rsem.at[K_G])

    def prepare_g(b, carry):
        halves(gs, b, block_of(g_recv, b).astype(F32))
        return carry

    lax.fori_loop(0, NBLK, prepare_g, 0)

    def interleave(b, first, count):
        for j in range(3):
            some = stack[b, pl.ds(3 * cap * first + j, cap * count, stride=3), :]
            rb_send[pl.ds(b * per_blk + first, count), :, j * LANES : (j + 1) * LANES] = (
                some.astype(BF16).reshape(count, cap, LANES)
            )

    def grads_of(i, carry):
        b = nth(i)
        chosen = chosen_of(b)
        pb = probs[b]
        p = pb.astype(F32)
        dp = nt(jnp.concatenate([block_of(v_recv, c) for c in chosen], 0), gs[b])
        delta = jnp.sum(p * dp, 0, keepdims=True)
        ds = (p * (dp - delta)).astype(BF16)
        gq_t = nn(jnp.concatenate([k_t[c] for c in chosen], 1), ds)
        gk_part[b, 0:KB] = nn(ds, qs[b]).reshape(KB, BLK, LANES)
        gv_part[b, 0:KB] = nn(pb, gs[b]).reshape(KB, BLK, LANES)
        gq = jnp.where(head_sub, gq_t[:, 0:BLK], gq_t[:, BLK : 2 * BLK]).T * 0.125
        stack[b, 0:BLK] = gq
        interleave(b, 0, 1)
        to_group(rb_send, rb_recv, K_BACK, b, range(1))
        return carry

    lax.fori_loop(0, NBLK, grads_of, 0)

    def key_side(i, carry):
        c = nth(i)
        gk = jnp.zeros((BLK, LANES), F32)
        gv = jnp.zeros((BLK, LANES), F32)
        for b in range(NBLK):
            j = jnp.int32(KB)
            for which in range(KB):
                j = jnp.where(pat_ref[which, b] == c, which, j)
            gk = gk + gk_part[b, j]
            gv = gv + gv_part[b, j]
        stack[c, BLK : 2 * BLK] = gk
        stack[c, 2 * BLK : 3 * BLK] = gv
        interleave(c, 1, per_blk - 1)
        to_group(rb_send, rb_recv, K_BACK, c, range(1, per_blk))
        return carry

    lax.fori_loop(0, NBLK, key_side, 0)
    rb_recv[me] = rb_send[me]

    wait_bytes(ra_recv.at[pl.ds(0, n - 1)], rsem.at[K_CTX])
    context = nn(pick[...], ra_recv[...].reshape(slots, LANES)).astype(BF16)
    u_send[...] = nn(context, wo_ref[...]).astype(BF16).reshape(tp, chunk, width)
    to_tp(lambda peer: u_send.at[peer], lambda at: u_recv.at[at], K_UPD)
    qkv_rows = 3 * width // n
    proj = nn(gout_t[...], context).astype(BF16)
    gw_send[:, qkv_rows:] = proj.reshape(n, width // n, LANES)

    mine = pl.ds(pl.multiple_of(tm * chunk, chunk), chunk)
    u_recv[tm] = u_send[tm]
    wait_bytes(u_recv.at[pl.ds(0, tp - 1)], rsem.at[K_UPD])
    update = jnp.sum(u_recv[...].astype(F32), 0).astype(BF16).astype(F32)
    o_all[tm] = (pts_ref[mine, :].astype(F32) + update).astype(BF16)
    to_tp(lambda peer: o_all.at[tm], lambda at: o_all.at[at], K_OUT)

    wait_bytes(rb_recv.at[pl.ds(0, n - 1)], rsem.at[K_BACK])
    back = nn(pick[...], rb_recv[...].reshape(slots, 3 * LANES)).astype(BF16)
    gq = back[:, 0:LANES]
    gk = back[:, LANES : 2 * LANES]
    gv = back[:, 2 * LANES : 3 * LANES]
    part = nt(gq, wqkv_ref[0]) + nt(gk, wqkv_ref[1]) + nt(gv, wqkv_ref[2])
    n_send[...] = part.astype(BF16).reshape(tp, chunk, width)
    parts = ((K_N0, K_I0, pl.ds(0, half)), (K_N1, K_I1, pl.ds(half, half)))
    for phase, _, at_half in parts:
        to_tp(
            lambda peer: n_send.at[peer, at_half], lambda at: n_recv.at[at, at_half], phase
        )
    nmt = normed_t[...]
    for j, g in enumerate((gq, gk, gv)):
        gw = nn(nmt, g).astype(BF16)
        for i in range(n):
            first, last = max(i * qkv_rows, j * width), min((i + 1) * qkv_rows, (j + 1) * width)
            if first < last:
                gw_send[i, first - i * qkv_rows : last - i * qkv_rows] = gw[
                    first - j * width : last - j * width
                ]
    to_pts(lambda peer: gw_send.at[peer], gw_recv, K_W)
    gain_part = jnp.sum(part * xhat[...], 0, keepdims=True)
    for j in range(width // LANES):
        gg_recv[me, j] = gain_part[:, j * LANES : (j + 1) * LANES]
    to_pts(lambda peer: gg_recv.at[me], gg_recv, K_GAIN)

    n_recv[tm] = n_send[tm]
    for which, (phase, phase_out, at_half) in enumerate(parts):
        wait_bytes(n_recv.at[pl.ds(0, tp - 1), at_half], rsem.at[phase])
        mine_half = pl.ds(pl.multiple_of(tm * chunk + which * half, half), half)
        grad = jnp.sum(n_recv[:, at_half].astype(F32), 0).astype(BF16).astype(F32)
        hat = xhat[mine_half, :]
        scaled = grad * gain_ref[...]
        first = jnp.mean(scaled, -1, keepdims=True)
        second = jnp.mean(scaled * hat, -1, keepdims=True)
        branch = inv_std[mine_half, :] * (scaled - first - hat * second)
        branch = branch.astype(BF16).astype(F32)
        i_all[tm, at_half] = (gout_ref[mine_half, :].astype(F32) + branch).astype(BF16)
        to_tp(
            lambda peer: i_all.at[tm, at_half], lambda at: i_all.at[at, at_half], phase_out
        )

    gw_recv[me] = gw_send[me]
    wait_bytes(gw_recv.at[pl.ds(0, n - 1)], rsem.at[K_W])
    gw_all[me] = jnp.sum(gw_recv[...].astype(F32), 0).astype(BF16)
    to_pts(lambda peer: gw_all.at[me], gw_all, K_WALL)

    wait_bytes(gg_recv.at[pl.ds(0, n - 1)], rsem.at[K_GAIN])
    gx_recv[tm] = jnp.sum(gg_recv[...], 0)
    to_tp(lambda peer: gx_recv.at[tm], lambda at: gx_recv.at[at], K_GAINX)

    wait_bytes(o_all.at[pl.ds(0, tp - 1)], rsem.at[K_OUT])
    out_ref[...] = o_all[...].reshape(points, width)
    wait_bytes(gw_all.at[pl.ds(0, n - 1)], rsem.at[K_WALL])
    gqkv_ref[...] = gw_all[:, 0:qkv_rows].astype(F32).reshape(gqkv_ref.shape)
    gproj_ref[...] = gw_all[:, qkv_rows:].astype(F32).reshape(width, LANES).T
    wait_bytes(gx_recv.at[pl.ds(0, tp - 1)], rsem.at[K_GAINX])
    gain_sum = jnp.sum(gx_recv[...], 0)
    for j in range(width // LANES):
        ggain_ref[:, j * LANES : (j + 1) * LANES] = gain_sum[j]
    for _, phase_out, at_half in parts:
        wait_bytes(i_all.at[pl.ds(0, tp - 1), at_half], rsem.at[phase_out])
    gin_ref[...] = i_all[...].reshape(points, width)

    for phase, buf in (
        (K_Q, kq_send),
        (K_V, v_send),
        (K_G, g_send),
        (K_CTX, ra_send),
        (K_BACK, rb_send),
        (K_W, gw_send),
        (K_GAIN, gg_recv),
        (K_WALL, gw_all),
    ):
        wait_bytes(buf.at[pl.ds(0, n - 1)], ssem.at[phase])
    for phase, buf in ((K_UPD, u_send), (K_OUT, o_all), (K_GAINX, gx_recv)):
        wait_bytes(buf.at[pl.ds(0, tp - 1)], ssem.at[phase])
    for phase, phase_out, at_half in parts:
        wait_bytes(n_send.at[pl.ds(0, tp - 1), at_half], ssem.at[phase])
        wait_bytes(i_all.at[pl.ds(0, tp - 1), at_half], ssem.at[phase_out])


def hand_out(*refs):
    count = len(refs) // 2
    sems = refs[-1]
    copies = [
        pltpu.make_async_copy(refs[i], refs[count + i], sems.at[i]) for i in range(count)
    ]
    for copy in copies:
        copy.start()
    for copy in copies:
        copy.wait()


def body(n, tp, points, destination, pattern, norm_gain, qkv_weight, out_weight, grad_out):
    rows, width = points.shape
    cap = 2 * rows // n
    slots = n * cap
    chunk = rows // tp
    wrows = 4 * width // n
    vm = pl.BlockSpec(memory_space=pltpu.VMEM)
    hbm = pl.BlockSpec(memory_space=pltpu.HBM)
    any_space = pl.BlockSpec(memory_space=pl.ANY)
    scratch = [
        pltpu.VMEM((rows, width), BF16),
        pltpu.VMEM((1, rows), jnp.int32),
        pltpu.SMEM((KB, NBLK), jnp.int32),
        pltpu.VMEM((1, width), F32),
        pltpu.VMEM((3, width, LANES), BF16),
        pltpu.VMEM((LANES, width), BF16),
        pltpu.VMEM((rows, width), BF16),
        pltpu.SemaphoreType.DMA((7,)),
        pltpu.VMEM((rows, width), F32),
        pltpu.VMEM((rows, 1), F32),
        pltpu.VMEM((rows, width), BF16),
        pltpu.VMEM((width, rows), BF16),
        pltpu.VMEM((width, rows), BF16),
        pltpu.VMEM((rows, slots), BF16),
        pltpu.VMEM((NBLK, BLK, rows), BF16),
        pltpu.VMEM((rows, 2 * LANES), BF16),
        pltpu.VMEM((rows, 2 * LANES), BF16),
        pltpu.VMEM((n, cap, 2 * LANES), BF16),
        pltpu.VMEM((n, cap, 2 * LANES), BF16),
        pltpu.VMEM((n, cap, LANES), BF16),
        pltpu.VMEM((n, cap, LANES), BF16),
        pltpu.VMEM((n, cap, LANES), BF16),
        pltpu.VMEM((n, cap, LANES), BF16),
        pltpu.VMEM((NBLK, 2 * BLK, LANES), BF16),
        pltpu.VMEM((NBLK, 2 * BLK, LANES), BF16),
        pltpu.VMEM((NBLK, LANES, BLK), BF16),
        pltpu.VMEM((NBLK, LANES, BLK), BF16),
        pltpu.VMEM((NBLK, BLK, LANES), F32),
        pltpu.VMEM((NBLK, KB * BLK, 2 * BLK), BF16),
        pltpu.VMEM((NBLK, KB + 1, BLK, LANES), F32),
        pltpu.VMEM((NBLK, KB + 1, BLK, LANES), F32),
        pltpu.VMEM((NBLK, 3 * BLK, LANES), F32),
        pltpu.VMEM((n, cap, LANES), BF16),
        pltpu.VMEM((n, cap, LANES), BF16),
        pltpu.VMEM((n, cap, 3 * LANES), BF16),
        pltpu.VMEM((n, cap, 3 * LANES), BF16),
        pltpu.VMEM((tp, chunk, width), BF16),
        pltpu.VMEM((tp, chunk, width), BF16),
        pltpu.VMEM((tp, chunk, width), BF16),
        pltpu.VMEM((tp, chunk, width), BF16),
        pltpu.VMEM((tp, chunk, width), BF16),
        pltpu.VMEM((tp, chunk, width), BF16),
        pltpu.VMEM((n, wrows, LANES), BF16),
        pltpu.VMEM((n, wrows, LANES), BF16),
        pltpu.VMEM((n, wrows, LANES), BF16),
        pltpu.VMEM((n, width // LANES, 1, LANES), F32),
        pltpu.VMEM((tp, width // LANES, 1, LANES), F32),
        pltpu.SemaphoreType.DMA((15,)),
        pltpu.SemaphoreType.DMA((15,)),
    ]
    shapes = (
        jax.ShapeDtypeStruct((rows, width), BF16),
        jax.ShapeDtypeStruct((rows, width), BF16),
        jax.ShapeDtypeStruct((3, width, LANES), F32),
        jax.ShapeDtypeStruct((LANES, width), F32),
        jax.ShapeDtypeStruct((1, width), F32),
    )
    results = pl.pallas_call(
        functools.partial(kernel, n, tp),
        out_shape=shapes,
        in_specs=[hbm] * 7,
        out_specs=(vm,) * 5,
        scratch_shapes=scratch,
        compiler_params=pltpu.CompilerParams(
            collective_id=0, has_side_effects=True, vmem_limit_bytes=VMEM_LIMIT
        ),
        name="point_attention",
    )(
        points,
        destination.reshape(1, rows),
        pattern.T,
        norm_gain.reshape(1, width),
        qkv_weight,
        out_weight,
        grad_out,
    )
    out, grad_input, grad_qkv, grad_proj, grad_gain = pl.pallas_call(
        hand_out,
        out_shape=shapes,
        in_specs=[vm] * 5,
        out_specs=(any_space,) * 5,
        scratch_shapes=[pltpu.SemaphoreType.DMA((5,))],
        compiler_params=pltpu.CompilerParams(vmem_limit_bytes=VMEM_LIMIT),
        name="hand_out",
    )(*results)
    return out, grad_input, grad_qkv, grad_proj, grad_gain.reshape(width)


def solution(mesh):
    return jax.shard_map(
        functools.partial(body, mesh.shape["pts"], mesh.shape["tp"]),
        mesh=mesh,
        in_specs=(
            P("pts", None),
            P("pts", None),
            P("pts", None),
            P(),
            P(None, None, "tp"),
            P("tp", None),
            P("pts", None),
        ),
        out_specs=(P("pts", None), P("pts", None), P(None, None, "tp"), P("tp", None), P()),
        check_vma=False,
    )
```

time: 81.4 us -> 70.1 us (0.86)
  local copies, waits for them, and re-layouts: 8.49 us -> 0 us
  Pallas kernels: 71.8 us -> 68.3 us
    unnamed x19 -> x0, local copies, waits for them, and re-layouts: 8.49 us -> none
    pallas_call x1 -> x2, Pallas kernels: 71.8 us -> 68.3 us  [the longest x1 65.4 us: body(): pl.pallas_call(functools.partial(kernel, n, tp), out_shape=shapes, in_spe...]
where the time goes in v2:
time: 70.1 us; the launch traced here: 68.9 us
  Pallas kernels  68.3 us (97%)
    pallas_call x1, Pallas kernels, body(): pl.pallas_call(functools.partial(kernel, n, tp), out_shape=shapes, in_spe...  65.4 us
    pallas_call x1, Pallas kernels, body(): pl.pallas_call(hand_out, out_shape=shapes, in_specs=[vm] * 5, out_specs=(...  2.89 us

profile of v2, /device:TPU:0, one launch (start us, length us, event | category | flops | bytes accessed | tf_op | source)
XLA Modules:
  0.0 68.9 jit_solution(1222521455390917701)
XLA Ops:
  0.6 65.4 %point_attention.1 = (bf16[512,512]{1,0:T(8,128)(2,1)}, bf16[512,512]{1,0:T(8,128)(2,1)}, f32[3,512,128]{2,1,0:T(8,128)}, f32[128,512]{1,0:T(8,128)}, f32[1,512]{1,0:T(1,128)}) custom-call(bf16[512,512]{1,0:T(8,128)(2,1)} %pts_hbm.1, s32[1,512]{1,0:T(1,128)} %bitcast.4, s32[4,8]{1,0:T(4,128)} %bitcast.5, f32[1,512]{1,0:T(1,128)} %bitcast.6, ...), custom_call_target="tpu_custom_call" | custom-call | tf_op jit(solution)/shard_map/point_attention/pallas_call | solution.py:569
  66.0 2.9 %hand_out.1 = (bf16[512,512]{1,0:T(8,128)(2,1)}, bf16[512,512]{1,0:T(8,128)(2,1)}, f32[3,512,128]{2,1,0:T(8,128)}, f32[128,512]{1,0:T(8,128)}, f32[1,512]{1,0:T(1,128)}) custom-call(bf16[512,512]{1,0:T(8,128)(2,1)} %get-tuple-element.15.refs_0_, bf16[512,512]{1,0:T(8,128)(2,1)} %get-tuple-element.16.refs_1_, f32[3,512,128]{2,1,0:T(8,128)} %get-tuple-element.17.refs_2_, ...), custom_call_target="tpu_custom_call" | custom-call | tf_op jit(solution)/shard_map/hand_out/pallas_call | solution.py:588

commit v3 on v2

v3 whole, which is shorter than its diff:
```python
import functools

import jax
import jax.numpy as jnp
from jax import lax
from jax.experimental import pallas as pl
from jax.experimental.pallas import tpu as pltpu
from jax.sharding import PartitionSpec as P

MESH = pl.DeviceIdType.MESH
F32 = jnp.float32
BF16 = jnp.bfloat16
BLK = 128
NBLK = 8
KB = 4
LANES = 128
HALF = 64
EMPTY = 2e38
EMPTY_CUT = 1e38
LOW = -1e30
VMEM_LIMIT = 60 * 1024 * 1024
YS, ZS, CORES = 4, 4, 2


def ring(step, size):
    return min(step, size - step)


OFFSETS = sorted(
    [(y, z, c) for y in range(YS) for z in range(ZS) for c in range(CORES)][1:],
    key=lambda o: (-ring(o[0], YS) - ring(o[1], ZS), o),
)

CHIPS = [(y, z) for y, z, c in OFFSETS if c == 0]

(K_Q, K_V, K_G, K_CTX, K_BACK, K_UPD, K_OUT, K_N, K_IN, K_W, K_WALL, K_GAIN, K_GAINX, K_WO, K_WQKV) = (
    0, 1, 2, 3, 4, 7, 8, 9, 12, 13, 14, 15, 16, 17, 18
)
K_PAIR, K_FORWARD, PHASES = 19, 23, 24


def nn(a, b):
    return jnp.dot(a, b, preferred_element_type=F32)


def nt(a, b):
    return lax.dot_general(a, b, (((1,), (1,)), ((), ())), preferred_element_type=F32)


def wait_bytes(ref, sem):
    pltpu.make_async_copy(ref, ref, sem).wait()


def kernel(
    n,
    tp,
    pts_hbm,
    dest_hbm,
    pat_hbm,
    gain_hbm,
    wqkv_hbm,
    wo_hbm,
    gout_hbm,
    out_hbm,
    gin_hbm,
    gw_hbm,
    ggain_hbm,
    pts_ref,
    dest_ref,
    pat_ref,
    gain_ref,
    wqkv_all,
    wo_all,
    gout_ref,
    in_sem,
    out_sem,
    xhat,
    inv_std,
    normed,
    normed_t,
    gout_t,
    pick,
    put_all,
    rows_kq,
    rows_vg,
    kq_send,
    kq_recv,
    v_send,
    v_recv,
    g_send,
    g_recv,
    qs,
    gs,
    k_t,
    v_t,
    bias,
    probs,
    gk_part,
    gv_part,
    stack,
    ra_send,
    ra_recv,
    rb_send,
    rb_recv,
    c_send,
    c_recv,
    n_send,
    n_recv,
    acc,
    acc_gain,
    o_all,
    i_all,
    pair_send,
    pair_recv,
    gw_send,
    gw_recv,
    gw_all,
    gg_recv,
    gx_recv,
    gain_out,
    ssem,
    rsem,
):
    me = lax.axis_index("pts")
    tm = lax.axis_index("tp")
    cap = kq_send.shape[1]
    per_blk = BLK // cap
    points, width = pts_ref.shape
    slots = n * cap
    chunk = points // tp
    my_y = me // (ZS * CORES)
    my_z = lax.rem(me // CORES, ZS)
    my_c = lax.rem(me, CORES)

    barrier = pltpu.get_barrier_semaphore()

    def greet(i, carry):
        pl.semaphore_signal(
            barrier, inc=1, device_id=(lax.rem(me + i, n), tm), device_id_type=MESH
        )
        return carry

    for i in range(1, tp):
        pl.semaphore_signal(
            barrier, inc=1, device_id=(me, lax.rem(tm + i, tp)), device_id_type=MESH
        )
    lax.fori_loop(1, n, greet, 0)

    fetches = [
        pltpu.make_async_copy(src, dst, in_sem.at[i])
        for i, (src, dst) in enumerate(
            (
                (dest_hbm, dest_ref),
                (pts_hbm, pts_ref),
                (gain_hbm, gain_ref),
                (wqkv_hbm, wqkv_all.at[tm]),
                (gout_hbm, gout_ref),
                (wo_hbm, wo_all.at[tm]),
                (pat_hbm, pat_ref),
            )
        )
    ]
    for fetch in fetches:
        fetch.start()

    def remote(src, dst, phase, peer):
        return pltpu.make_async_remote_copy(
            src_ref=src,
            dst_ref=dst,
            send_sem=ssem.at[phase],
            recv_sem=rsem.at[phase],
            device_id=peer,
            device_id_type=MESH,
        )

    def to_pts(send, recv, phase):
        for dy, dz, dc in OFFSETS:
            peer = (lax.rem(my_y + dy, YS) * ZS + lax.rem(my_z + dz, ZS)) * CORES
            peer = peer + lax.rem(my_c + dc, CORES)
            remote(send(peer), recv.at[me], phase, (peer, tm)).start()

    chips = n // CORES
    my_chip = me // CORES
    twin = (me + 1 - 2 * my_c, tm)

    def to_chips(send, recv, phase):
        for dy, dz in CHIPS:
            chip = lax.rem(my_y + dy, YS) * ZS + lax.rem(my_z + dz, ZS)
            remote(send(chip), recv.at[my_chip], phase, (chip * CORES + my_c, tm)).start()

    def pair(which, rows):
        pair_send[which] = rows.reshape(pair_send.shape[1:])
        remote(
            pair_send.at[which, 1 - my_c], pair_recv.at[which], K_PAIR + which, twin
        ).start()

    def fold(which):
        wait_bytes(pair_recv.at[which], rsem.at[K_PAIR + which])
        both = pair_send[which, my_c].astype(F32) + pair_recv[which].astype(F32)
        gw_send[:, which] = both.astype(BF16).reshape(chips, width // n, LANES)

    def to_tp(send, recv, phase):
        for i in range(1, tp):
            peer = lax.rem(tm + i, tp)
            remote(send(peer), recv(tm), phase, (me, peer)).start()

    def nth(i):
        dy = jnp.where(i < 2, 2, jnp.where(i < 6, 1 + 2 * lax.rem(i, 2), 0))
        dz = jnp.where(i < 2, 1 - i, jnp.where(i < 6, 1 - (i - 2) // 2, 7 - i))
        return lax.rem(my_y + dy, YS) * 2 + lax.rem(my_z // 2 + dz, 2)

    def blocks(step, work, order=None):
        def some(i, carry):
            at = [i * step + k for k in range(step)]
            work([order(a) for a in at] if order else at)
            return carry

        lax.fori_loop(0, NBLK // step, some, 0)

    def to_group(send, recv, phase, b, which):
        for u in which:
            peer = b * per_blk + u

            @pl.when(peer != me)
            def _():
                remote(send.at[peer], recv.at[me], phase, (peer, tm)).start()

    upto = jnp.where(
        lax.broadcasted_iota(jnp.int32, (points, points), 0)
        <= lax.broadcasted_iota(jnp.int32, (points, points), 1),
        1.0,
        0.0,
    ).astype(BF16)
    fetches[0].wait()
    dest = dest_ref[...].astype(F32)
    owner = lax.broadcasted_iota(jnp.int32, (n, points), 0).astype(F32)
    onehot = jnp.where(dest == owner, 1.0, 0.0)
    count = nn(onehot.astype(BF16), upto)
    index = dest * cap + jnp.sum(count * onehot, 0, keepdims=True) - 1.0

    fetches[1].wait()
    fetches[2].wait()

    def norm(r, carry):
        at = pl.ds(pl.multiple_of(r * BLK, BLK), BLK)
        x = pts_ref[at, :].astype(F32)
        shifted = x - jnp.mean(x, -1, keepdims=True)
        inv = lax.rsqrt(jnp.mean(shifted * shifted, -1, keepdims=True) + 1e-05)
        hat = shifted * inv
        xhat[at, :] = hat
        inv_std[at, :] = inv
        normed[at, :] = (hat * gain_ref[...]).astype(BF16)
        return carry

    lax.fori_loop(0, points // BLK, norm, 0)
    fetches[3].wait()
    nm = normed[...]
    rows_kq[:, 0:LANES] = nn(nm, wqkv_all[tm, 1]).astype(BF16)
    rows_kq[:, LANES : 2 * LANES] = (nn(nm, wqkv_all[tm, 0]).astype(BF16).astype(F32) * 0.125).astype(
        BF16
    )
    slot_sub = lax.broadcasted_iota(jnp.int32, (BLK, points), 0).astype(F32)
    ones = jnp.ones((points, LANES), BF16)

    pl.semaphore_wait(barrier, n - 1 + tp - 1)

    def place(some):
        puts = [
            jnp.where(slot_sub + (c * BLK).astype(F32) == index, 1.0, 0.0).astype(BF16)
            for c in some
        ]
        lives = [nn(put, ones) for put in puts]
        kqs = [nn(put, rows_kq[...]) for put in puts]
        for c, put, live, kq in zip(some, puts, lives, kqs):
            put_all[c] = put
            k = kq[:, 0:LANES].astype(BF16)
            q = jnp.where(live > 0.5, kq[:, LANES : 2 * LANES], EMPTY).astype(BF16)
            at = pl.ds(c * per_blk, per_blk)
            kq_send[at, :, 0:LANES] = k.reshape(per_blk, cap, LANES)
            kq_send[at, :, LANES : 2 * LANES] = q.reshape(per_blk, cap, LANES)
        for c in some:
            to_group(kq_send, kq_recv, K_Q, c, range(per_blk))

    blocks(2, place, nth)
    kq_recv[me] = kq_send[me]

    fetches[4].wait()
    fetches[5].wait()
    to_tp(lambda peer: wo_all.at[tm], lambda at: wo_all.at[at], K_WO)
    to_tp(lambda peer: wqkv_all.at[tm], lambda at: wqkv_all.at[at], K_WQKV)
    rows_vg[:, 0:LANES] = nn(nm, wqkv_all[tm, 2]).astype(BF16)
    rows_vg[:, LANES : 2 * LANES] = nt(gout_ref[...], wo_all[tm]).astype(BF16)

    def place_more(some):
        vgs = [nn(put_all[c], rows_vg[...]).astype(BF16) for c in some]
        for c, vg in zip(some, vgs):
            at = pl.ds(c * per_blk, per_blk)
            v_send[at] = vg[:, 0:LANES].reshape(per_blk, cap, LANES)
            g_send[at] = vg[:, LANES : 2 * LANES].reshape(per_blk, cap, LANES)
        for c in some:
            to_group(v_send, v_recv, K_V, c, range(per_blk))

    blocks(4, place_more, nth)
    to_pts(lambda peer: g_send.at[peer], g_recv, K_G)
    v_recv[me] = v_send[me]
    g_recv[me] = g_send[me]

    fetches[6].wait()
    index_col = jnp.broadcast_to(index, (LANES, points)).T
    lane = lax.broadcasted_iota(jnp.int32, (points, LANES), 1).astype(F32)
    for t in range(slots // LANES):
        pick[:, t * LANES : (t + 1) * LANES] = jnp.where(
            index_col == lane + t * LANES, 1.0, 0.0
        ).astype(BF16)
    normed_t[...] = nm.astype(F32).T.astype(BF16)
    gout_t[...] = gout_ref[...].astype(F32).T.astype(BF16)
    gk_part[:, KB] = jnp.zeros((NBLK, BLK, LANES), F32)
    gv_part[:, KB] = jnp.zeros((NBLK, BLK, LANES), F32)

    head_lane = lax.broadcasted_iota(jnp.int32, (BLK, LANES), 1) < HALF
    head_sub = lax.broadcasted_iota(jnp.int32, (LANES, BLK), 0) < HALF

    def block_of(ref, b, first=0):
        return ref[pl.ds(b * per_blk, per_blk), :, first : first + LANES].reshape(BLK, LANES)

    def halves(ref, b, rows):
        ref[b, 0:BLK] = jnp.where(head_lane, rows, 0.0).astype(BF16)
        ref[b, BLK : 2 * BLK] = jnp.where(head_lane, 0.0, rows).astype(BF16)

    def chosen_of(b):
        return [pat_ref[j, b] for j in range(KB)]

    wait_bytes(kq_recv.at[pl.ds(0, n - 1)], rsem.at[K_Q])

    def prepare(some):
        for b in some:
            q = block_of(kq_recv, b, LANES).astype(F32)
            empty = q > EMPTY_CUT
            bias[b] = jnp.where(empty, LOW, 0.0)
            halves(qs, b, jnp.where(empty, 0.0, q))
            k_t[b] = block_of(kq_recv, b).astype(F32).T.astype(BF16)

    blocks(8, prepare)

    def softmax(some):
        scores = []
        for b in some:
            chosen = chosen_of(b)
            keys = jnp.concatenate([block_of(kq_recv, c) for c in chosen], 0)
            low = jnp.concatenate([bias[c] for c in chosen], 0)
            scores.append(nt(keys, qs[b]) + jnp.concatenate([low, low], 1))
        for b, score in zip(some, scores):
            raised = jnp.exp(score - jnp.max(score, 0, keepdims=True))
            p = raised * (1.0 / jnp.sum(raised, 0, keepdims=True))
            probs[b] = p.astype(BF16)

    blocks(8, softmax)

    wait_bytes(v_recv.at[pl.ds(0, n - 1)], rsem.at[K_V])

    def prepare_v(some):
        for b in some:
            v_t[b] = block_of(v_recv, b).astype(F32).T.astype(BF16)

    blocks(8, prepare_v)

    def mix(some):
        ctx_t = [
            nn(jnp.concatenate([v_t[c] for c in chosen_of(b)], 1), probs[b]) for b in some
        ]
        ctx = [jnp.where(head_sub, c[:, 0:BLK], c[:, BLK : 2 * BLK]).T.astype(BF16) for c in ctx_t]
        for b, c in zip(some, ctx):
            ra_send[pl.ds(b * per_blk, per_blk)] = c.reshape(per_blk, cap, LANES)
        for b in some:
            to_group(ra_send, ra_recv, K_CTX, b, range(per_blk))

    blocks(8, mix, nth)
    ra_recv[me] = ra_send[me]

    wait_bytes(g_recv.at[pl.ds(0, n - 1)], rsem.at[K_G])

    def prepare_g(some):
        for b in some:
            halves(gs, b, block_of(g_recv, b).astype(F32))

    blocks(8, prepare_g)

    def interleave(b, first, count):
        for j in range(3):
            some = stack[b, pl.ds(3 * cap * first + j, cap * count, stride=3), :]
            rb_send[j, pl.ds(b * per_blk + first, count)] = some.astype(BF16).reshape(
                count, cap, LANES
            )

    def grads_of(some):
        dps = [
            nt(jnp.concatenate([block_of(v_recv, c) for c in chosen_of(b)], 0), gs[b])
            for b in some
        ]
        dss = []
        for b, dp in zip(some, dps):
            gv_part[b, 0:KB] = nn(probs[b], gs[b]).reshape(KB, BLK, LANES)
            p = probs[b].astype(F32)
            delta = jnp.sum(p * dp, 0, keepdims=True)
            dss.append((p * (dp - delta)).astype(BF16))
        gqs = []
        for b, ds in zip(some, dss):
            gq_t = nn(jnp.concatenate([k_t[c] for c in chosen_of(b)], 1), ds)
            gk_part[b, 0:KB] = nn(ds, qs[b]).reshape(KB, BLK, LANES)
            gqs.append(jnp.where(head_sub, gq_t[:, 0:BLK], gq_t[:, BLK : 2 * BLK]).T * 0.125)
        for b, gq in zip(some, gqs):
            stack[b, 0:BLK] = gq
        for b in some:
            interleave(b, 0, 1)
        for b in some:
            for j in range(3):
                to_group(rb_send.at[j], rb_recv.at[j], K_BACK + j, b, range(1))

    blocks(8, grads_of, nth)

    def key_side(some):
        for c in some:
            gk = jnp.zeros((BLK, LANES), F32)
            gv = jnp.zeros((BLK, LANES), F32)
            for b in range(NBLK):
                j = jnp.int32(KB)
                for which in range(KB):
                    j = jnp.where(pat_ref[which, b] == c, which, j)
                gk = gk + gk_part[b, j]
                gv = gv + gv_part[b, j]
            stack[c, BLK : 2 * BLK] = gk
            stack[c, 2 * BLK : 3 * BLK] = gv
        for c in some:
            interleave(c, 1, per_blk - 1)
        for c in some:
            to_group(rb_send.at[0], rb_recv.at[0], K_BACK, c, range(1, per_blk))

    blocks(8, key_side, nth)

    def send_slab(j):
        def one(i, carry):
            to_group(rb_send.at[j], rb_recv.at[j], K_BACK + j, nth(i), range(1, per_blk))
            return carry

        lax.fori_loop(0, NBLK, one, 0)

    send_slab(1)
    send_slab(2)
    for j in range(3):
        rb_recv[j, me] = rb_send[j, me]

    wait_bytes(ra_recv.at[pl.ds(0, n - 1)], rsem.at[K_CTX])
    context = nn(pick[...], ra_recv[...].reshape(slots, LANES)).astype(BF16)
    c_send[...] = context.reshape(tp, chunk, LANES)
    to_tp(lambda peer: c_send.at[peer], lambda at: c_recv.at[at], K_UPD)

    pair(3, nn(gout_t[...], c_send[...].reshape(points, LANES)).astype(BF16))
    c_recv[tm] = c_send[tm]
    wait_bytes(wo_all.at[pl.ds(0, tp - 1)], rsem.at[K_WO])
    wait_bytes(c_recv.at[pl.ds(0, tp - 1)], rsem.at[K_UPD])
    mine = pl.ds(pl.multiple_of(tm * chunk, chunk), chunk)
    update = sum(nn(c_recv[t], wo_all[t]) for t in range(tp)).astype(BF16).astype(F32)
    o_all[tm] = (pts_ref[mine, :].astype(F32) + update).astype(BF16)
    to_tp(lambda peer: o_all.at[tm], lambda at: o_all.at[at], K_OUT)
    wait_bytes(wqkv_all.at[pl.ds(0, tp - 1)], rsem.at[K_WQKV])

    acc[...] = jnp.zeros_like(acc)

    def add_rows(j):
        n_recv[j, tm] = n_send[j, tm]
        wait_bytes(n_recv.at[j, pl.ds(0, tp - 1)], rsem.at[K_N + j])
        acc[...] += sum(nt(n_recv[j, t], wqkv_all[t, j]) for t in range(tp))

    for j in range(3):
        wait_bytes(rb_recv.at[j, pl.ds(0, n - 1)], rsem.at[K_BACK + j])
        rows = nn(pick[...], rb_recv[j].reshape(slots, LANES)).astype(BF16)
        n_send[j] = rows.reshape(tp, chunk, LANES)
        to_tp(lambda peer: n_send.at[j, peer], lambda at: n_recv.at[j, at], K_N + j)
        gw = nn(normed_t[...], rows)
        pair(j, gw.astype(BF16))
        weighted = gw * wqkv_all[tm, j].astype(F32)
        acc_gain[...] = weighted if j == 0 else acc_gain[...] + weighted
    gain_part = jnp.sum(acc_gain[...].T, 0, keepdims=True) / gain_ref[...]
    for j in range(width // LANES):
        gg_recv[me, j] = gain_part[:, j * LANES : (j + 1) * LANES]
    to_pts(lambda peer: gg_recv.at[me], gg_recv, K_GAIN)
    for which in (3, 0, 1, 2):
        fold(which)
    to_chips(lambda chip: gw_send.at[chip], gw_recv, K_W)

    add_rows(0)
    add_rows(1)
    wait_bytes(gg_recv.at[pl.ds(0, n - 1)], rsem.at[K_GAIN])
    gx_recv[tm] = jnp.sum(gg_recv[...], 0)
    to_tp(lambda peer: gx_recv.at[tm], lambda at: gx_recv.at[at], K_GAINX)
    add_rows(2)
    grad = acc[...]
    grad = grad.astype(BF16).astype(F32)
    hat = xhat[mine, :]
    scaled = grad * gain_ref[...]
    first = jnp.mean(scaled, -1, keepdims=True)
    second = jnp.mean(scaled * hat, -1, keepdims=True)
    branch = (inv_std[mine, :] * (scaled - first - hat * second)).astype(BF16).astype(F32)
    i_all[tm] = (gout_ref[mine, :].astype(F32) + branch).astype(BF16)
    to_tp(lambda peer: i_all.at[tm], lambda at: i_all.at[at], K_IN)

    gw_recv[my_chip] = gw_send[my_chip]
    wait_bytes(gw_recv.at[pl.ds(0, chips - 1)], rsem.at[K_W])
    gw_all[my_c, my_chip] = jnp.sum(gw_recv[...].astype(F32), 0).astype(BF16)
    to_chips(lambda chip: gw_all.at[my_c, my_chip], gw_all.at[my_c], K_WALL)

    def hand(src, dst, which):
        copy = pltpu.make_async_copy(src, dst, out_sem.at[which])
        copy.start()
        return copy

    wait_bytes(o_all.at[pl.ds(0, tp - 1)], rsem.at[K_OUT])
    handed = [hand(o_all, out_hbm, 0)]

    for phase, buf in (
        (K_Q, kq_send),
        (K_V, v_send),
        (K_G, g_send),
        (K_CTX, ra_send),
        (K_BACK, rb_send.at[0]),
        (K_BACK + 1, rb_send.at[1]),
        (K_BACK + 2, rb_send.at[2]),
        (K_GAIN, gg_recv),
    ):
        wait_bytes(buf.at[pl.ds(0, n - 1)], ssem.at[phase])
    for phase, buf in (
        (K_WO, wo_all),
        (K_WQKV, wqkv_all),
        (K_UPD, c_send),
        (K_OUT, o_all),
        (K_N, n_send.at[0]),
        (K_N + 1, n_send.at[1]),
        (K_N + 2, n_send.at[2]),
    ):
        wait_bytes(buf.at[pl.ds(0, tp - 1)], ssem.at[phase])

    wait_bytes(gw_all.at[my_c, pl.ds(0, chips - 1)], rsem.at[K_WALL])
    remote(gw_all.at[my_c], gw_all.at[my_c], K_FORWARD, twin).start()
    wait_bytes(gx_recv.at[pl.ds(0, tp - 1)], rsem.at[K_GAINX])
    gain_sum = jnp.sum(gx_recv[...], 0)
    for j in range(width // LANES):
        gain_out[:, j * LANES : (j + 1) * LANES] = gain_sum[j]
    handed.append(hand(gain_out, ggain_hbm, 1))
    wait_bytes(i_all.at[pl.ds(0, tp - 1)], rsem.at[K_IN])
    handed.append(hand(i_all, gin_hbm, 2))
    wait_bytes(gw_all.at[1 - my_c], rsem.at[K_FORWARD])
    handed.append(hand(gw_all, gw_hbm, 3))
    for phase, buf in ((K_IN, i_all), (K_GAINX, gx_recv)):
        wait_bytes(buf.at[pl.ds(0, tp - 1)], ssem.at[phase])
    wait_bytes(gw_send.at[pl.ds(0, chips - 1)], ssem.at[K_W])
    wait_bytes(gw_all.at[my_c, pl.ds(0, chips - 1)], ssem.at[K_WALL])
    wait_bytes(gw_all.at[my_c], ssem.at[K_FORWARD])
    for which in range(4):
        wait_bytes(pair_recv.at[which], ssem.at[K_PAIR + which])
    for copy in handed:
        copy.wait()


def hand_out(
    out_in,
    gin_in,
    gw_in,
    gain_in,
    out_ref,
    gin_ref,
    gqkv_ref,
    gproj_ref,
    gain_ref,
    out_buf,
    gin_buf,
    gw_buf,
    gain_buf,
    gqkv_buf,
    gproj_buf,
    sems,
):
    def copy(src, dst, which):
        one = pltpu.make_async_copy(src, dst, sems.at[which])
        one.start()
        return one

    gw_get = copy(gw_in, gw_buf, 0)
    out_get = copy(out_in, out_buf, 1)
    gin_get = copy(gin_in, gin_buf, 2)
    gain_get = copy(gain_in, gain_buf, 3)
    width = out_buf.shape[1]

    def whole(which):
        return gw_buf[:, :, which].reshape(width, LANES).astype(F32)

    puts = []
    gw_get.wait()
    for j in range(3):
        gqkv_buf[j] = whole(j)
    puts.append(copy(gqkv_buf, gqkv_ref, 4))
    out_get.wait()
    puts.append(copy(out_buf, out_ref, 5))
    gin_get.wait()
    puts.append(copy(gin_buf, gin_ref, 6))
    gproj_buf[...] = whole(3).T
    puts.append(copy(gproj_buf, gproj_ref, 7))
    gain_get.wait()
    puts.append(copy(gain_buf, gain_ref, 8))
    for put in puts:
        put.wait()


def body(n, tp, points, destination, pattern, norm_gain, qkv_weight, out_weight, grad_out):
    rows, width = points.shape
    cap = 2 * rows // n
    slots = n * cap
    chunk = rows // tp
    hbm = pl.BlockSpec(memory_space=pltpu.HBM)
    scratch = [
        pltpu.VMEM((rows, width), BF16),
        pltpu.VMEM((1, rows), jnp.int32),
        pltpu.SMEM((KB, NBLK), jnp.int32),
        pltpu.VMEM((1, width), F32),
        pltpu.VMEM((tp, 3, width, LANES), BF16),
        pltpu.VMEM((tp, LANES, width), BF16),
        pltpu.VMEM((rows, width), BF16),
        pltpu.SemaphoreType.DMA((7,)),
        pltpu.SemaphoreType.DMA((4,)),
        pltpu.VMEM((rows, width), F32),
        pltpu.VMEM((rows, 1), F32),
        pltpu.VMEM((rows, width), BF16),
        pltpu.VMEM((width, rows), BF16),
        pltpu.VMEM((width, rows), BF16),
        pltpu.VMEM((rows, slots), BF16),
        pltpu.VMEM((NBLK, BLK, rows), BF16),
        pltpu.VMEM((rows, 2 * LANES), BF16),
        pltpu.VMEM((rows, 2 * LANES), BF16),
        pltpu.VMEM((n, cap, 2 * LANES), BF16),
        pltpu.VMEM((n, cap, 2 * LANES), BF16),
        pltpu.VMEM((n, cap, LANES), BF16),
        pltpu.VMEM((n, cap, LANES), BF16),
        pltpu.VMEM((n, cap, LANES), BF16),
        pltpu.VMEM((n, cap, LANES), BF16),
        pltpu.VMEM((NBLK, 2 * BLK, LANES), BF16),
        pltpu.VMEM((NBLK, 2 * BLK, LANES), BF16),
        pltpu.VMEM((NBLK, LANES, BLK), BF16),
        pltpu.VMEM((NBLK, LANES, BLK), BF16),
        pltpu.VMEM((NBLK, BLK, LANES), F32),
        pltpu.VMEM((NBLK, KB * BLK, 2 * BLK), BF16),
        pltpu.VMEM((NBLK, KB + 1, BLK, LANES), F32),
        pltpu.VMEM((NBLK, KB + 1, BLK, LANES), F32),
        pltpu.VMEM((NBLK, 3 * BLK, LANES), F32),
        pltpu.VMEM((n, cap, LANES), BF16),
        pltpu.VMEM((n, cap, LANES), BF16),
        pltpu.VMEM((3, n, cap, LANES), BF16),
        pltpu.VMEM((3, n, cap, LANES), BF16),
        pltpu.VMEM((tp, chunk, LANES), BF16),
        pltpu.VMEM((tp, chunk, LANES), BF16),
        pltpu.VMEM((3, tp, chunk, LANES), BF16),
        pltpu.VMEM((3, tp, chunk, LANES), BF16),
        pltpu.VMEM((chunk, width), F32),
        pltpu.VMEM((width, LANES), F32),
        pltpu.VMEM((tp, chunk, width), BF16),
        pltpu.VMEM((tp, chunk, width), BF16),
        pltpu.VMEM((4, CORES, width // CORES, LANES), BF16),
        pltpu.VMEM((4, width // CORES, LANES), BF16),
        pltpu.VMEM((n // CORES, 4, width // n, LANES), BF16),
        pltpu.VMEM((n // CORES, 4, width // n, LANES), BF16),
        pltpu.VMEM((CORES, n // CORES, 4, width // n, LANES), BF16),
        pltpu.VMEM((n, width // LANES, 1, LANES), F32),
        pltpu.VMEM((tp, width // LANES, 1, LANES), F32),
        pltpu.VMEM((1, width), F32),
        pltpu.SemaphoreType.DMA((PHASES,)),
        pltpu.SemaphoreType.DMA((PHASES,)),
    ]
    out_shape = jax.ShapeDtypeStruct((rows, width), BF16)
    gain_shape = jax.ShapeDtypeStruct((1, width), F32)
    qkv_shape = jax.ShapeDtypeStruct((3, width, LANES), F32)
    proj_shape = jax.ShapeDtypeStruct((LANES, width), F32)
    by_tp = jax.ShapeDtypeStruct((tp, chunk, width), BF16)
    parts = jax.ShapeDtypeStruct((CORES, n // CORES, 4, width // n, LANES), BF16)
    out, grad_input, grads, gain = pl.pallas_call(
        functools.partial(kernel, n, tp),
        out_shape=(by_tp, by_tp, parts, gain_shape),
        in_specs=[hbm] * 7,
        out_specs=(hbm,) * 4,
        scratch_shapes=scratch,
        compiler_params=pltpu.CompilerParams(
            collective_id=0, has_side_effects=True, vmem_limit_bytes=VMEM_LIMIT
        ),
        name="point_attention",
    )(
        points,
        destination.reshape(1, rows),
        pattern.T,
        norm_gain.reshape(1, width),
        qkv_weight,
        out_weight,
        grad_out,
    )
    out, grad_input, grad_qkv, grad_proj, grad_gain = pl.pallas_call(
        hand_out,
        out_shape=(out_shape, out_shape, qkv_shape, proj_shape, gain_shape),
        in_specs=[hbm] * 4,
        out_specs=(hbm,) * 5,
        scratch_shapes=[
            pltpu.VMEM((rows, width), BF16),
            pltpu.VMEM((rows, width), BF16),
            pltpu.VMEM((CORES, n // CORES, 4, width // n, LANES), BF16),
            pltpu.VMEM((1, width), F32),
            pltpu.VMEM((3, width, LANES), F32),
            pltpu.VMEM((LANES, width), F32),
            pltpu.SemaphoreType.DMA((9,)),
        ],
        compiler_params=pltpu.CompilerParams(vmem_limit_bytes=VMEM_LIMIT),
        name="hand_out",
    )(out.reshape(rows, width), grad_input.reshape(rows, width), grads, gain)
    return out, grad_input, grad_qkv, grad_proj, grad_gain.reshape(width)


def solution(mesh):
    return jax.shard_map(
        functools.partial(body, mesh.shape["pts"], mesh.shape["tp"]),
        mesh=mesh,
        in_specs=(
            P("pts", None),
            P("pts", None),
            P("pts", None),
            P(),
            P(None, None, "tp"),
            P("tp", None),
            P("pts", None),
        ),
        out_specs=(P("pts", None), P("pts", None), P(None, None, "tp"), P("tp", None), P()),
        check_vma=False,
    )
```

time: 70.1 us -> 61.8 us (0.88); the launches traced: 68.9 us -> 61.7 us
  Pallas kernels: 68.3 us -> 60.9 us
    pallas_call x2, Pallas kernels: 68.3 us -> 60.9 us  [the longest x1 58.4 us: body(): pl.pallas_call(functools.partial(kernel, n, tp), out_shape=(by_tp, by_tp,...]
where the time goes in v3:
time: 61.8 us; the launch traced here: 61.7 us
  Pallas kernels  60.9 us (99%)
  between operations  0.8 us (1%)
    pallas_call x1, Pallas kernels, body(): pl.pallas_call(functools.partial(kernel, n, tp), out_shape=(by_tp, by_tp,...  58.4 us
    pallas_call x1, Pallas kernels, body(): pl.pallas_call(hand_out, out_shape=(out_shape, out_shape, qkv_shape, proj...  2.48 us

profile of v3, /device:TPU:0, one launch (start us, length us, event | category | flops | bytes accessed | tf_op | source)
XLA Modules:
  0.0 61.7 jit_solution(5737585206042127043)
XLA Ops:
  0.6 58.4 %point_attention.1 = (bf16[4,128,512]{2,1,0:T(8,128)(2,1)}, bf16[4,128,512]{2,1,0:T(8,128)(2,1)}, bf16[2,16,4,16,128]{4,3,2,1,0:T(8,128)(2,1)}, f32[1,512]{1,0:T(1,128)}) custom-call(bf16[512,512]{1,0:T(8,128)(2,1)} %pts_hbm.1, s32[1,512]{1,0:T(1,128)} %bitcast.8, s32[4,8]{1,0:T(4,128)} %bitcast.9, f32[1,512]{1,0:T(1,128)} %bitcast.10, ...), custom_call_target="tpu_custom_call" | custom-call | tf_op jit(solution)/shard_map/point_attention/pallas_call | solution.py:682
  59.0 2.5 %hand_out.1 = (bf16[512,512]{1,0:T(8,128)(2,1)}, bf16[512,512]{1,0:T(8,128)(2,1)}, f32[3,512,128]{2,1,0:T(8,128)}, f32[128,512]{1,0:T(8,128)}, f32[1,512]{1,0:T(1,128)}) custom-call(bf16[512,512]{1,0:T(8,128)(2,1)} %bitcast.6, bf16[512,512]{1,0:T(8,128)(2,1)} %bitcast.7, bf16[2,16,4,16,128]{4,3,2,1,0:T(8,128)(2,1)} %get-tuple-element.16.gw_in, ...), custom_call_target="tpu_custom_call" | custom-call | tf_op jit(solution)/shard_map/hand_out/pallas_call | solution.py:701

commit v4 on v3

--- a/solution.py
+++ b/solution.py
@@ -36,7 +36,7 @@
 (K_Q, K_V, K_G, K_CTX, K_BACK, K_UPD, K_OUT, K_N, K_IN, K_W, K_WALL, K_GAIN, K_GAINX, K_WO, K_WQKV) = (
     0, 1, 2, 3, 4, 7, 8, 9, 12, 13, 14, 15, 16, 17, 18
 )
-K_PAIR, K_FORWARD, PHASES = 19, 23, 24
+K_PAIR, K_FORWARD, K_OUT_REST, K_GAIN_PAIR, PHASES = 19, 23, 24, 25, 26
 
 
 def nn(a, b):
@@ -115,6 +115,8 @@
     gw_send,
     gw_recv,
     gw_all,
+    gg_own,
+    gg_twin,
     gg_recv,
     gx_recv,
     gain_out,
@@ -461,7 +463,12 @@
     mine = pl.ds(pl.multiple_of(tm * chunk, chunk), chunk)
     update = sum(nn(c_recv[t], wo_all[t]) for t in range(tp)).astype(BF16).astype(F32)
     o_all[tm] = (pts_ref[mine, :].astype(F32) + update).astype(BF16)
-    to_tp(lambda peer: o_all.at[tm], lambda at: o_all.at[at], K_OUT)
+    out_parts = ((K_OUT, pl.ds(0, chunk // 2)), (K_OUT_REST, pl.ds(chunk // 2, chunk // 2)))
+
+    def send_out(which):
+        phase, part = out_parts[which]
+        to_tp(lambda peer: o_all.at[tm, part], lambda at: o_all.at[at, part], phase)
+
     wait_bytes(wqkv_all.at[pl.ds(0, tp - 1)], rsem.at[K_WQKV])
 
     acc[...] = jnp.zeros_like(acc)
@@ -476,21 +483,26 @@
         rows = nn(pick[...], rb_recv[j].reshape(slots, LANES)).astype(BF16)
         n_send[j] = rows.reshape(tp, chunk, LANES)
         to_tp(lambda peer: n_send.at[j, peer], lambda at: n_recv.at[j, at], K_N + j)
+        if j != 1:
+            send_out(j // 2)
         gw = nn(normed_t[...], rows)
         pair(j, gw.astype(BF16))
         weighted = gw * wqkv_all[tm, j].astype(F32)
         acc_gain[...] = weighted if j == 0 else acc_gain[...] + weighted
     gain_part = jnp.sum(acc_gain[...].T, 0, keepdims=True) / gain_ref[...]
     for j in range(width // LANES):
-        gg_recv[me, j] = gain_part[:, j * LANES : (j + 1) * LANES]
-    to_pts(lambda peer: gg_recv.at[me], gg_recv, K_GAIN)
+        gg_own[j] = gain_part[:, j * LANES : (j + 1) * LANES]
+    remote(gg_own, gg_twin, K_GAIN_PAIR, twin).start()
     for which in (3, 0, 1, 2):
         fold(which)
+    wait_bytes(gg_twin, rsem.at[K_GAIN_PAIR])
+    gg_recv[my_chip] = gg_own[...] + gg_twin[...]
+    to_chips(lambda chip: gg_recv.at[my_chip], gg_recv, K_GAIN)
     to_chips(lambda chip: gw_send.at[chip], gw_recv, K_W)
 
     add_rows(0)
     add_rows(1)
-    wait_bytes(gg_recv.at[pl.ds(0, n - 1)], rsem.at[K_GAIN])
+    wait_bytes(gg_recv.at[pl.ds(0, chips - 1)], rsem.at[K_GAIN])
     gx_recv[tm] = jnp.sum(gg_recv[...], 0)
     to_tp(lambda peer: gx_recv.at[tm], lambda at: gx_recv.at[at], K_GAINX)
     add_rows(2)
@@ -514,7 +526,8 @@
         copy.start()
         return copy
 
-    wait_bytes(o_all.at[pl.ds(0, tp - 1)], rsem.at[K_OUT])
+    for phase, part in out_parts:
+        wait_bytes(o_all.at[pl.ds(0, tp - 1), part], rsem.at[phase])
     handed = [hand(o_all, out_hbm, 0)]
 
     for phase, buf in (
@@ -525,14 +538,12 @@
         (K_BACK, rb_send.at[0]),
         (K_BACK + 1, rb_send.at[1]),
         (K_BACK + 2, rb_send.at[2]),
-        (K_GAIN, gg_recv),
     ):
         wait_bytes(buf.at[pl.ds(0, n - 1)], ssem.at[phase])
     for phase, buf in (
         (K_WO, wo_all),
         (K_WQKV, wqkv_all),
         (K_UPD, c_send),
-        (K_OUT, o_all),
         (K_N, n_send.at[0]),
         (K_N + 1, n_send.at[1]),
         (K_N + 2, n_send.at[2]),
@@ -541,6 +552,8 @@
 
     wait_bytes(gw_all.at[my_c, pl.ds(0, chips - 1)], rsem.at[K_WALL])
     remote(gw_all.at[my_c], gw_all.at[my_c], K_FORWARD, twin).start()
+    for phase, part in out_parts:
+        wait_bytes(o_all.at[pl.ds(0, tp - 1), part], ssem.at[phase])
     wait_bytes(gx_recv.at[pl.ds(0, tp - 1)], rsem.at[K_GAINX])
     gain_sum = jnp.sum(gx_recv[...], 0)
     for j in range(width // LANES):
@@ -552,6 +565,8 @@
     handed.append(hand(gw_all, gw_hbm, 3))
     for phase, buf in ((K_IN, i_all), (K_GAINX, gx_recv)):
         wait_bytes(buf.at[pl.ds(0, tp - 1)], ssem.at[phase])
+    wait_bytes(gg_own, ssem.at[K_GAIN_PAIR])
+    wait_bytes(gg_recv.at[pl.ds(0, chips - 1)], ssem.at[K_GAIN])
     wait_bytes(gw_send.at[pl.ds(0, chips - 1)], ssem.at[K_W])
     wait_bytes(gw_all.at[my_c, pl.ds(0, chips - 1)], ssem.at[K_WALL])
     wait_bytes(gw_all.at[my_c], ssem.at[K_FORWARD])
@@ -584,11 +599,17 @@
         one.start()
         return one
 
+    rows, width = out_buf.shape
     gw_get = copy(gw_in, gw_buf, 0)
-    out_get = copy(out_in, out_buf, 1)
-    gin_get = copy(gin_in, gin_buf, 2)
-    gain_get = copy(gain_in, gain_buf, 3)
-    width = out_buf.shape[1]
+    halves = []
+    for i, (src, buf, dst) in enumerate(
+        ((out_in, out_buf, out_ref), (gin_in, gin_buf, gin_ref))
+    ):
+        for k in range(2):
+            part = pl.ds(k * rows // 2, rows // 2)
+            get = copy(src.at[part], buf.at[part], 1 + 2 * i + k)
+            halves.append((get, buf.at[part], dst.at[part], 5 + 2 * i + k))
+    gain_get = copy(gain_in, gain_buf, 9)
 
     def whole(which):
         return gw_buf[:, :, which].reshape(width, LANES).astype(F32)
@@ -597,15 +618,14 @@
     gw_get.wait()
     for j in range(3):
         gqkv_buf[j] = whole(j)
-    puts.append(copy(gqkv_buf, gqkv_ref, 4))
-    out_get.wait()
-    puts.append(copy(out_buf, out_ref, 5))
-    gin_get.wait()
-    puts.append(copy(gin_buf, gin_ref, 6))
+    puts.append(copy(gqkv_buf, gqkv_ref, 10))
+    for get, src, dst, sem in halves:
+        get.wait()
+        puts.append(copy(src, dst, sem))
     gproj_buf[...] = whole(3).T
-    puts.append(copy(gproj_buf, gproj_ref, 7))
+    puts.append(copy(gproj_buf, gproj_ref, 11))
     gain_get.wait()
-    puts.append(copy(gain_buf, gain_ref, 8))
+    puts.append(copy(gain_buf, gain_ref, 12))
     for put in puts:
         put.wait()
 
@@ -667,7 +687,9 @@
         pltpu.VMEM((n // CORES, 4, width // n, LANES), BF16),
         pltpu.VMEM((n // CORES, 4, width // n, LANES), BF16),
         pltpu.VMEM((CORES, n // CORES, 4, width // n, LANES), BF16),
-        pltpu.VMEM((n, width // LANES, 1, LANES), F32),
+        pltpu.VMEM((width // LANES, 1, LANES), F32),
+        pltpu.VMEM((width // LANES, 1, LANES), F32),
+        pltpu.VMEM((n // CORES, width // LANES, 1, LANES), F32),
         pltpu.VMEM((tp, width // LANES, 1, LANES), F32),
         pltpu.VMEM((1, width), F32),
         pltpu.SemaphoreType.DMA((PHASES,)),
@@ -710,7 +732,7 @@
             pltpu.VMEM((1, width), F32),
             pltpu.VMEM((3, width, LANES), F32),
             pltpu.VMEM((LANES, width), F32),
-            pltpu.SemaphoreType.DMA((9,)),
+            pltpu.SemaphoreType.DMA((13,)),
         ],
         compiler_params=pltpu.CompilerParams(vmem_limit_bytes=VMEM_LIMIT),
         name="hand_out",

time: 61.8 us -> 60.5 us (0.979)
  Pallas kernels: 60.9 us -> 59.6 us
    pallas_call x1, Pallas kernels: 58.4 us -> 57.1 us  [body(): pl.pallas_call(functools.partial(kernel, n, tp), out_shape=(by_tp, by_tp,...]
where the time goes in v4:
time: 60.5 us; the launch traced here: 60.4 us
  Pallas kernels  59.6 us (99%)
  between operations  0.8 us (1%)
    pallas_call x1, Pallas kernels, body(): pl.pallas_call(functools.partial(kernel, n, tp), out_shape=(by_tp, by_tp,...  57.1 us
    pallas_call x1, Pallas kernels, body(): pl.pallas_call(hand_out, out_shape=(out_shape, out_shape, qkv_shape, proj...  2.52 us

profile of v4, /device:TPU:0, one launch (start us, length us, event | category | flops | bytes accessed | tf_op | source)
XLA Modules:
  0.0 60.4 jit_solution(5266759234889054655)
XLA Ops:
  0.6 57.1 %point_attention.1 = (bf16[4,128,512]{2,1,0:T(8,128)(2,1)}, bf16[4,128,512]{2,1,0:T(8,128)(2,1)}, bf16[2,16,4,16,128]{4,3,2,1,0:T(8,128)(2,1)}, f32[1,512]{1,0:T(1,128)}) custom-call(bf16[512,512]{1,0:T(8,128)(2,1)} %pts_hbm.1, s32[1,512]{1,0:T(1,128)} %bitcast.8, s32[4,8]{1,0:T(4,128)} %bitcast.9, f32[1,512]{1,0:T(1,128)} %bitcast.10, ...), custom_call_target="tpu_custom_call" | custom-call | tf_op jit(solution)/shard_map/point_attention/pallas_call | solution.py:704
  57.7 2.5 %hand_out.1 = (bf16[512,512]{1,0:T(8,128)(2,1)}, bf16[512,512]{1,0:T(8,128)(2,1)}, f32[3,512,128]{2,1,0:T(8,128)}, f32[128,512]{1,0:T(8,128)}, f32[1,512]{1,0:T(1,128)}) custom-call(bf16[512,512]{1,0:T(8,128)(2,1)} %bitcast.6, bf16[512,512]{1,0:T(8,128)(2,1)} %bitcast.7, bf16[2,16,4,16,128]{4,3,2,1,0:T(8,128)(2,1)} %get-tuple-element.16.gw_in, ...), custom_call_target="tpu_custom_call" | custom-call | tf_op jit(solution)/shard_map/hand_out/pallas_call | solution.py:723

commit v5 on v4

--- a/solution.py
+++ b/solution.py
@@ -33,10 +33,10 @@
 
 CHIPS = [(y, z) for y, z, c in OFFSETS if c == 0]
 
-(K_Q, K_V, K_G, K_CTX, K_BACK, K_UPD, K_OUT, K_N, K_IN, K_W, K_WALL, K_GAIN, K_GAINX, K_WO, K_WQKV) = (
-    0, 1, 2, 3, 4, 7, 8, 9, 12, 13, 14, 15, 16, 17, 18
+(K_Q, K_V, K_G, K_CTX, K_BACK, K_UPD, K_OUT, K_N, K_IN, K_W, K_GAIN, K_GAINX, K_WO, K_WQKV) = (
+    0, 1, 2, 3, 4, 7, 8, 9, 12, 13, 15, 16, 17, 18
 )
-K_PAIR, K_FORWARD, K_OUT_REST, K_GAIN_PAIR, PHASES = 19, 23, 24, 25, 26
+K_PAIR, K_FORWARD, K_OUT_REST, K_GAIN_PAIR, K_CHIPS, PHASES = 19, 26, 24, 25, 28, 30
 
 
 def nn(a, b):
@@ -134,20 +134,6 @@
     my_z = lax.rem(me // CORES, ZS)
     my_c = lax.rem(me, CORES)
 
-    barrier = pltpu.get_barrier_semaphore()
-
-    def greet(i, carry):
-        pl.semaphore_signal(
-            barrier, inc=1, device_id=(lax.rem(me + i, n), tm), device_id_type=MESH
-        )
-        return carry
-
-    for i in range(1, tp):
-        pl.semaphore_signal(
-            barrier, inc=1, device_id=(me, lax.rem(tm + i, tp)), device_id_type=MESH
-        )
-    lax.fori_loop(1, n, greet, 0)
-
     fetches = [
         pltpu.make_async_copy(src, dst, in_sem.at[i])
         for i, (src, dst) in enumerate(
@@ -165,6 +151,20 @@
     for fetch in fetches:
         fetch.start()
 
+    barrier = pltpu.get_barrier_semaphore()
+
+    def greet(i, carry):
+        pl.semaphore_signal(
+            barrier, inc=1, device_id=(lax.rem(me + i, n), tm), device_id_type=MESH
+        )
+        return carry
+
+    for i in range(1, tp):
+        pl.semaphore_signal(
+            barrier, inc=1, device_id=(me, lax.rem(tm + i, tp)), device_id_type=MESH
+        )
+    lax.fori_loop(1, n, greet, 0)
+
     def remote(src, dst, phase, peer):
         return pltpu.make_async_remote_copy(
             src_ref=src,
@@ -243,8 +243,8 @@
     fetches[1].wait()
     fetches[2].wait()
 
-    def norm(r, carry):
-        at = pl.ds(pl.multiple_of(r * BLK, BLK), BLK)
+    for r in range(points // BLK):
+        at = pl.ds(r * BLK, BLK)
         x = pts_ref[at, :].astype(F32)
         shifted = x - jnp.mean(x, -1, keepdims=True)
         inv = lax.rsqrt(jnp.mean(shifted * shifted, -1, keepdims=True) + 1e-05)
@@ -252,9 +252,7 @@
         xhat[at, :] = hat
         inv_std[at, :] = inv
         normed[at, :] = (hat * gain_ref[...]).astype(BF16)
-        return carry
-
-    lax.fori_loop(0, points // BLK, norm, 0)
+
     fetches[3].wait()
     nm = normed[...]
     rows_kq[:, 0:LANES] = nn(nm, wqkv_all[tm, 1]).astype(BF16)
@@ -437,7 +435,7 @@
         for c in some:
             to_group(rb_send.at[0], rb_recv.at[0], K_BACK, c, range(1, per_blk))
 
-    blocks(8, key_side, nth)
+    blocks(4, key_side, nth)
 
     def send_slab(j):
         def one(i, carry):
@@ -469,6 +467,7 @@
         phase, part = out_parts[which]
         to_tp(lambda peer: o_all.at[tm, part], lambda at: o_all.at[at, part], phase)
 
+    send_out(0)
     wait_bytes(wqkv_all.at[pl.ds(0, tp - 1)], rsem.at[K_WQKV])
 
     acc[...] = jnp.zeros_like(acc)
@@ -483,8 +482,8 @@
         rows = nn(pick[...], rb_recv[j].reshape(slots, LANES)).astype(BF16)
         n_send[j] = rows.reshape(tp, chunk, LANES)
         to_tp(lambda peer: n_send.at[j, peer], lambda at: n_recv.at[j, at], K_N + j)
-        if j != 1:
-            send_out(j // 2)
+        if j == 2:
+            send_out(1)
         gw = nn(normed_t[...], rows)
         pair(j, gw.astype(BF16))
         weighted = gw * wqkv_all[tm, j].astype(F32)
@@ -516,10 +515,11 @@
     i_all[tm] = (gout_ref[mine, :].astype(F32) + branch).astype(BF16)
     to_tp(lambda peer: i_all.at[tm], lambda at: i_all.at[at], K_IN)
 
+    part_chips = chips // 2
     gw_recv[my_chip] = gw_send[my_chip]
     wait_bytes(gw_recv.at[pl.ds(0, chips - 1)], rsem.at[K_W])
     gw_all[my_c, my_chip] = jnp.sum(gw_recv[...].astype(F32), 0).astype(BF16)
-    to_chips(lambda chip: gw_all.at[my_c, my_chip], gw_all.at[my_c], K_WALL)
+    to_chips(lambda chip: gw_all.at[my_c, my_chip], gw_all.at[my_c], K_CHIPS + my_chip // part_chips)
 
     def hand(src, dst, which):
         copy = pltpu.make_async_copy(src, dst, out_sem.at[which])
@@ -550,8 +550,18 @@
     ):
         wait_bytes(buf.at[pl.ds(0, tp - 1)], ssem.at[phase])
 
-    wait_bytes(gw_all.at[my_c, pl.ds(0, chips - 1)], rsem.at[K_WALL])
-    remote(gw_all.at[my_c], gw_all.at[my_c], K_FORWARD, twin).start()
+    for h in range(2):
+
+        @pl.when(my_chip // part_chips == h)
+        def _():
+            wait_bytes(gw_all.at[my_c, pl.ds(0, part_chips - 1)], rsem.at[K_CHIPS + h])
+
+        @pl.when(my_chip // part_chips != h)
+        def _():
+            wait_bytes(gw_all.at[my_c, pl.ds(0, part_chips)], rsem.at[K_CHIPS + h])
+
+        some = gw_all.at[my_c, pl.ds(h * part_chips, part_chips)]
+        remote(some, some, K_FORWARD + h, twin).start()
     for phase, part in out_parts:
         wait_bytes(o_all.at[pl.ds(0, tp - 1), part], ssem.at[phase])
     wait_bytes(gx_recv.at[pl.ds(0, tp - 1)], rsem.at[K_GAINX])
@@ -561,15 +571,17 @@
     handed.append(hand(gain_out, ggain_hbm, 1))
     wait_bytes(i_all.at[pl.ds(0, tp - 1)], rsem.at[K_IN])
     handed.append(hand(i_all, gin_hbm, 2))
-    wait_bytes(gw_all.at[1 - my_c], rsem.at[K_FORWARD])
+    for h in range(2):
+        wait_bytes(gw_all.at[1 - my_c, pl.ds(h * part_chips, part_chips)], rsem.at[K_FORWARD + h])
     handed.append(hand(gw_all, gw_hbm, 3))
     for phase, buf in ((K_IN, i_all), (K_GAINX, gx_recv)):
         wait_bytes(buf.at[pl.ds(0, tp - 1)], ssem.at[phase])
     wait_bytes(gg_own, ssem.at[K_GAIN_PAIR])
     wait_bytes(gg_recv.at[pl.ds(0, chips - 1)], ssem.at[K_GAIN])
     wait_bytes(gw_send.at[pl.ds(0, chips - 1)], ssem.at[K_W])
-    wait_bytes(gw_all.at[my_c, pl.ds(0, chips - 1)], ssem.at[K_WALL])
-    wait_bytes(gw_all.at[my_c], ssem.at[K_FORWARD])
+    wait_bytes(gw_all.at[my_c, pl.ds(0, chips - 1)], ssem.at[K_CHIPS + my_chip // part_chips])
+    for h in range(2):
+        wait_bytes(gw_all.at[my_c, pl.ds(h * part_chips, part_chips)], ssem.at[K_FORWARD + h])
     for which in range(4):
         wait_bytes(pair_recv.at[which], ssem.at[K_PAIR + which])
     for copy in handed:

time: 60.5 us -> 60.3 us (level)
  the two profiles are of different devices: /device:TPU:0 before, /device:TPU:1 now
where the time goes in v5:
time: 60.3 us; the launch traced here: 60.1 us
  Pallas kernels  59.3 us (98%)
  between operations  0.8 us (1%)
    pallas_call x1, Pallas kernels, body(): pl.pallas_call(functools.partial(kernel, n, tp), out_shape=(by_tp, by_tp,...  56.8 us
    pallas_call x1, Pallas kernels, body(): pl.pallas_call(hand_out, out_shape=(out_shape, out_shape, qkv_shape, proj...  2.52 us

profile of v5, /device:TPU:1, one launch (start us, length us, event | category | flops | bytes accessed | tf_op | source)
XLA Modules:
  0.0 60.1 jit_solution(18279030818337152765)
XLA Ops:
  0.6 56.8 %point_attention.1 = (bf16[4,128,512]{2,1,0:T(8,128)(2,1)}, bf16[4,128,512]{2,1,0:T(8,128)(2,1)}, bf16[2,16,4,16,128]{4,3,2,1,0:T(8,128)(2,1)}, f32[1,512]{1,0:T(1,128)}) custom-call(bf16[512,512]{1,0:T(8,128)(2,1)} %pts_hbm.1, s32[1,512]{1,0:T(1,128)} %bitcast.8, s32[4,8]{1,0:T(4,128)} %bitcast.9, f32[1,512]{1,0:T(1,128)} %bitcast.10, ...), custom_call_target="tpu_custom_call" | custom-call | tf_op jit(solution)/shard_map/point_attention/pallas_call | solution.py:716
  57.4 2.5 %hand_out.1 = (bf16[512,512]{1,0:T(8,128)(2,1)}, bf16[512,512]{1,0:T(8,128)(2,1)}, f32[3,512,128]{2,1,0:T(8,128)}, f32[128,512]{1,0:T(8,128)}, f32[1,512]{1,0:T(1,128)}) custom-call(bf16[512,512]{1,0:T(8,128)(2,1)} %bitcast.6, bf16[512,512]{1,0:T(8,128)(2,1)} %bitcast.7, bf16[2,16,4,16,128]{4,3,2,1,0:T(8,128)(2,1)} %get-tuple-element.16.gw_in, ...), custom_call_target="tpu_custom_call" | custom-call | tf_op jit(solution)/shard_map/hand_out/pallas_call | solution.py:735
